TPU v7x, 256 devices: a whole 4x4x8 slice. The times are simulated.
256 devices in a mesh: section: 8 (over y, x_lo), expert: 32 (over x_hi, z, core).
Axes of the slice: x: 4 (x_hi: 2, x_lo: 2; x = x_hi * 2 + x_lo), y: 4, z: 8, core: 2. Of those that a mesh axis runs over, the one named last changes fastest.
Arguments:
- tokens: bfloat16 [8, 512, 7168], P('section', 'expert'), may hold values from -6 to 6
- expert_ids: int32 [8, 512, 2], P('section', 'expert'), may hold values from 0 to 3, all different within a row; in each aligned block of 16 rows (0 to 15, 16 to 31, ..., all dimensions but the last counted through in order) at most 12 rows name the same one
- gate_values: float32 [8, 512, 2], P('section', 'expert'), may hold values from 0.3 to 1.5
- w_gate: bfloat16 [8, 7168, 4096], P('section', None, 'expert'), may hold values from -0.0625 to 0.0625
- w_up: bfloat16 [8, 7168, 4096], P('section', None, 'expert'), may hold values from -0.0625 to 0.0625
- w_down: bfloat16 [8, 4096, 7168], P('section', 'expert'), may hold values from -0.1875 to 0.1875
- norm_gain: float32 [8, 7168], P('section'), may hold values from 0.1 to 1.9
- w_dq: bfloat16 [8, 7168, 1536], P('section', 'expert'), may hold values from -0.0625 to 0.0625
- w_dkv: bfloat16 [8, 7168, 576], P('section', 'expert'), may hold values from -0.0625 to 0.0625
- q_gain: float32 [8, 1536], P('section'), may hold values from 0.1 to 1.9
- kv_gain: float32 [8, 512], P('section'), may hold values from 0.1 to 1.9
- w_uq: bfloat16 [8, 1536, 12288], P('section', None, 'expert'), may hold values from -0.15625 to 0.15625
- w_uk: bfloat16 [8, 64, 128, 512], P('section', 'expert'), may hold values from -3 to 3
- w_uv: bfloat16 [8, 64, 512, 128], P('section', 'expert'), may hold values from -0.25 to 0.25
- prefix_cache: bfloat16 [8, 2048, 576], P('section', 'expert'), may hold values from -8 to 8
Outputs:
- attended: bfloat16 [8, 512, 8192], P('section', None, 'expert')
Inputs may be any that keep to these rules, and one draw needn't show every extreme that they name: `expert_ids`: A token's 2 experts differ. Among the 16 tokens of one device (aligned blocks of rows) at most 12 entries name one expert, and in every draw some block reaches 12.
All inputs are finite; a program needn't handle non-finite values.
Results may differ from a plain program's by a relative error of at most 0.039.
Values may be sent and summed in bfloat16 or wider, within the bound.
A program may use at most 128 MiB of HBM per device.

v0:
```python
import jax
import jax.numpy as jnp
from jax import lax
from jax.sharding import PartitionSpec as P

EXPERTS = 4
ROPE = 64
NOPE = 128


EPSILON = 1e-06


def passed_along(block, axis, distance):
    devices = range(lax.axis_size(axis))
    route = [((i - distance) % len(devices), i) for i in devices]
    return lax.ppermute(block, axis, route)


def rms_apply(values, gain_row):
    mean_square = jnp.mean(values * values, axis=-1, keepdims=True)
    return values * lax.rsqrt(mean_square + EPSILON) * gain_row


def rotate(values, positions):
    half_width = values.shape[-1] // 2
    frequency = 10000.0 ** (-jnp.arange(half_width).astype(jnp.float32) / half_width)
    angles = positions.astype(jnp.float32)[:, None] * frequency[None, :]
    angles = angles.reshape((angles.shape[0],) + (1,) * (values.ndim - 2) + (half_width,))
    cosine = jnp.cos(angles)
    sine_part = jnp.sin(angles)
    leading = values[..., :half_width]
    trailing = values[..., half_width:]
    return jnp.concatenate(
        [leading * cosine - trailing * sine_part, leading * sine_part + trailing * cosine], axis=-1
    )


def finish_latent(latent, q_gain, kv_gain, positions):
    query_width = q_gain.shape[-1]
    key_width = kv_gain.shape[-1]
    query_part = rms_apply(latent[:, :query_width], q_gain)
    key_part = rms_apply(latent[:, query_width : query_width + key_width], kv_gain)
    rope_part = rotate(latent[:, query_width + key_width :], positions)
    return jnp.concatenate([query_part, key_part, rope_part], axis=1).astype(jnp.bfloat16)


def placement(flat_ids, chosen, capacity):
    matches = (flat_ids[..., None, :] == chosen[:, None]).astype(jnp.int32)
    earlier = jnp.cumsum(matches, axis=-1) - matches
    slot_index = jnp.arange(capacity)
    return matches[..., None, :] * (earlier[..., None, :] == slot_index[:, None]).astype(jnp.int32)


def per_device(
    tokens,
    expert_ids,
    gate_values,
    w_gate,
    w_up,
    w_down,
    norm_gain,
    w_dq,
    w_dkv,
    q_gain,
    kv_gain,
    w_uq,
    w_uk,
    w_uv,
    prefix_cache,
):
    own_tokens = tokens[0]
    routed_ids = expert_ids[0]
    gate_weights = gate_values[0]
    tok_dev, model_width = own_tokens.shape
    top_count = routed_ids.shape[1]
    devices = lax.axis_size("expert")
    group_size = devices // EXPERTS
    capacity = 3 * tok_dev // 4
    hidden_gate = w_gate[0]
    hidden_up = w_up[0]
    hidden_down = w_down[0]
    own_table = placement(routed_ids.reshape(-1), jnp.arange(EXPERTS), capacity)
    token_table = own_table.reshape(EXPERTS, capacity, tok_dev, top_count)
    gate_table = jnp.sum(token_table.astype(jnp.float32) * gate_weights[None, None], axis=-1)
    dispatch_table = jnp.sum(token_table, axis=-1).astype(jnp.bfloat16)
    outgoing = jnp.einsum(
        "ect,td->ecd", dispatch_table, own_tokens, preferred_element_type=jnp.float32
    ).astype(jnp.bfloat16)
    outgoing = jnp.repeat(outgoing, group_size, axis=0)
    slot_rows = lax.all_to_all(outgoing, "expert", split_axis=0, concat_axis=0, tiled=True)
    sources = slot_rows.shape[0]
    slot_count = slot_rows.shape[1]
    flat_rows = slot_rows.reshape(sources * slot_count, model_width)
    gate_part = jnp.dot(flat_rows, hidden_gate, preferred_element_type=jnp.float32)
    up_part = jnp.dot(flat_rows, hidden_up, preferred_element_type=jnp.float32)
    hidden = (jax.nn.silu(gate_part) * up_part).astype(jnp.bfloat16)
    partial_value = jnp.dot(hidden, hidden_down, preferred_element_type=jnp.float32).astype(
        jnp.bfloat16
    )
    returned = lax.all_to_all(
        partial_value.reshape(sources, slot_count, model_width),
        "expert",
        split_axis=0,
        concat_axis=0,
        tiled=True,
    )
    per_expert = jnp.sum(
        returned.reshape(EXPERTS, group_size, capacity, model_width).astype(jnp.float32), axis=1
    )
    combined = own_tokens.astype(jnp.float32) + jnp.einsum(
        "ect,ecd->td", gate_table, per_expert, precision=lax.Precision.HIGHEST
    )
    mixed = combined.astype(jnp.bfloat16)
    arriving = passed_along(mixed, "section", 1)
    normed = rms_apply(arriving.astype(jnp.float32), norm_gain[0]).astype(jnp.bfloat16)
    columns = lax.all_to_all(normed, "expert", split_axis=1, concat_axis=0, tiled=True)
    tokens_all = columns.shape[0]
    cache_len = prefix_cache.shape[1] * devices
    down_query = w_dq[0]
    down_keys = w_dkv[0]
    query_gain = q_gain[0]
    key_gain = kv_gain[0]
    positions = cache_len + jnp.arange(tokens_all)
    summed = lax.psum(
        jnp.concatenate(
            [
                jnp.dot(columns, down_query, preferred_element_type=jnp.float32),
                jnp.dot(columns, down_keys, preferred_element_type=jnp.float32),
            ],
            axis=1,
        ),
        "expert",
    )
    latent_rows = finish_latent(summed, query_gain, key_gain, positions)
    cached = lax.all_gather(prefix_cache[0], "expert", axis=0, tiled=True)
    query_width = query_gain.shape[-1]
    key_width = key_gain.shape[-1]
    key_rows = jnp.concatenate([cached, latent_rows[:, query_width:]], axis=0)
    query_rows = jnp.dot(latent_rows[:, :query_width], w_uq[0], preferred_element_type=jnp.float32)
    heads_dev = w_uk.shape[1]
    query_rows = query_rows.reshape(tokens_all, heads_dev, NOPE + ROPE)
    heads_nope = query_rows[..., :NOPE].astype(jnp.bfloat16)
    heads_rope = rotate(query_rows[..., NOPE:], positions).astype(jnp.bfloat16)
    absorbed = jnp.einsum(
        "thn,hnc->htc", heads_nope, w_uk[0], preferred_element_type=jnp.float32
    ).astype(jnp.bfloat16)
    queries = jnp.concatenate([absorbed, jnp.transpose(heads_rope, (1, 0, 2))], axis=-1)
    scores = jnp.einsum("htc,kc->htk", queries, key_rows, preferred_element_type=jnp.float32) * (
        NOPE + ROPE
    ) ** (-0.5)
    visible = jnp.arange(key_rows.shape[0])[None, :] <= positions[:, None]
    scores = jnp.where(visible[None], scores, -jnp.inf)
    weights = jax.nn.softmax(scores, axis=-1).astype(jnp.bfloat16)
    mixed_latent = jnp.einsum(
        "htk,kc->htc", weights, key_rows[:, :key_width], preferred_element_type=jnp.float32
    ).astype(jnp.bfloat16)
    output = jnp.einsum(
        "htc,hcv->thv", mixed_latent, w_uv[0], preferred_element_type=jnp.float32
    ).astype(jnp.bfloat16)
    return output.reshape(tokens_all, heads_dev * output.shape[-1])[None]


def solution(mesh):
    placed = (
        P("section", "expert", None),
        P("section", "expert", None),
        P("section", "expert", None),
        P("section", None, "expert"),
        P("section", None, "expert"),
        P("section", "expert", None),
        P("section", None),
        P("section", "expert", None),
        P("section", "expert", None),
        P("section", None),
        P("section", None),
        P("section", None, "expert"),
        P("section", "expert", None, None),
        P("section", "expert", None, None),
        P("section", "expert", None),
    )
    return jax.shard_map(
        per_device,
        mesh=mesh,
        in_specs=placed,
        out_specs=P("section", None, "expert"),
        check_vma=False,
    )
```

profile of v0, /device:TPU:1, one launch (start us, length us, event | category | flops | bytes accessed | tf_op | source)
XLA Modules:
  0.0 763.6 jit_solution(7832974037861141297)
XLA Ops:
  11.9 175.1 %all_to_all.29 = bf16[32,12,7168]{2,1,0:T(8,128)(2,1)} all-to-all(bf16[32,12,7168]{2,1,0:T(8,128)(2,1)S(1)} %bitcast.82), channel_id=1, replica_groups=mesh['section'=8,'expert'=32] {'expert'}, dimensions={0} | all-to-all | bytes 11010048 | tf_op jit(solution)/shard_map/all_to_all | solution.py:91
  186.9 8.2 %reshape.204 = bf16[384,7168]{1,0:T(8,128)(2,1)} reshape(bf16[32,12,7168]{2,1,0:T(8,128)(2,1)} %all_to_all.29) | data formatting | bytes 11010048 | tf_op jit(solution)/shard_map/reshape | solution.py:94
  195.2 4.7 fusion.13
  199.9 11.5 %convolution_convert_fusion = bf16[384,7168]{1,0:T(8,128)(2,1)} fusion(bf16[1,128,7168]{2,1,0:T(8,128)(2,1)S(1)} %copy-done, bf16[384,7168]{1,0:T(8,128)(2,1)} %reshape.204, bf16[1,7168,128]{2,1,0:T(8,128)(2,1)} %param.19, f32[384,128]{1,0:T(8,128)S(1)} %fusion.13), kind=kOutput, calls=%fused_computation.5 | convolution fusion | flops 1412333568 | bytes 14876672 | tf_op jit(solution)/shard_map/dot_general | solution.py:98
  211.3 8.0 %reshape.205 = bf16[32,12,7168]{2,1,0:T(8,128)(2,1)} reshape(bf16[384,7168]{1,0:T(8,128)(2,1)} %convolution_convert_fusion) | data formatting | bytes 11010048 | tf_op jit(solution)/shard_map/reshape | solution.py:102
  219.3 7.0 all-to-all-start.1
  227.2 171.7 %all-to-all-done.1 = bf16[32,12,7168]{2,1,0:T(8,128)(2,1)} async-done(((bf16[32,12,7168]{2,1,0:T(8,128)(2,1)}), bf16[32,12,7168]{2,1,0:T(8,128)(2,1)}, u32[]{:S(2)}, u32[]{:S(2)}) %all-to-all-start.1) | async-done | bytes 5505056 | tf_op jit(solution)/shard_map/all_to_all | solution.py:101
  398.9 4.5 convert_reduce_fusion
  405.1 6.6 collective-permute-done
  412.6 24.9 %all_to_all.30 = bf16[16,32,224]{2,0,1:T(8,128)(2,1)S(1)} all-to-all(bf16[16,32,224]{2,0,1:T(8,128)(2,1)S(1)} %copy.89), channel_id=1, replica_groups=mesh['section'=8,'expert'=32] {'expert'}, dimensions={1} | all-to-all | bytes 458752 | tf_op jit(solution)/shard_map/all_to_all | solution.py:117
  438.5 2.6 pad_maximum_fusion
  442.3 1.4 copy.91
  444.6 4.4 copy.95
  449.0 263.8 %all-reduce.2.cloned.1.call-done = f32[512,2112]{0,1:T(8,128)} async-done(((f32[512,2112]{0,1:T(8,128)}), f32[512,2112]{0,1:T(8,128)}) %all-reduce.2.cloned.1.call-update) | async-done | bytes 4325392 | tf_op jit(solution)/shard_map/psum | solution.py:125
  712.8 1.3 multiply_reduce_fusion.1
  714.2 2.2 multiply_reduce_fusion
  716.4 2.8 fusion.16
  719.7 1.4 multiply_cosine_fusion
  721.2 1.4 multiply_convert_fusion.1
  722.6 11.7 %maximum_maximum_fusion = bf16[2560,576]{0,1:T(8,128)(2,1)} fusion(bf16[512,32]{0,1:T(8,128)(2,1)S(1)} %get-tuple-element.11, bf16[512,32]{0,1:T(8,128)(2,1)S(1)} %get-tuple-element.12, bf16[512,512]{0,1:T(8,128)(2,1)S(1)} %multiply_convert_fusion.1, bf16[2048,576]{0,1:T(8,128)(2,1)S(1)} %bitcast.83), kind=kLoop, calls=%fused_computation.19 | loop fusion | flops 11796480 | bytes 5898240 | tf_op jit(solution)/shard_map/concatenate | solution.py:139
  734.2 4.3 fusion.8
  738.6 4.0 copy-done.13
  742.6 3.3 fusion.66
  745.9 10.1 %fusion.22 = bf16[2,512,128]{1,2,0:T(8,128)(2,1)S(1)} fusion(bf16[2560,576]{0,1:T(8,128)(2,1)} %maximum_maximum_fusion, f32[2,512]{1,0:T(2,128)S(1)} %fusion.66, f32[2,512,2560]{2,1,0:T(8,128)} %copy-done.13, pred[512,2560]{1,0:T(8,128)(4,1)S(1)} %iota_compare_fusion, bf16[1,2,512,128]{3,2,1,0:T(8,128)(2,1)} %param.28), kind=kOutput, calls=%fused_computation.35 | convolution fusion | flops 2832338432 | bytes 14946304 | tf_op jit(solution)/shard_map/htc,hcv->thv/dot_general | solution.py:158
  (67 shorter events, 13.1 us)
Async XLA Ops:
  6.5 193.3 %copy-start = (bf16[1,128,7168]{2,1,0:T(8,128)(2,1)S(1)}, bf16[1,128,7168]{2,1,0:T(8,128)(2,1)}, u32[]{:S(2)}) copy-start(bf16[1,128,7168]{2,1,0:T(8,128)(2,1)} %param.20) | copy-start | bytes 5505028
  219.3 7.8 %copy-start.12 = (f32[1,16,2]{1,2,0:T(2,128)S(1)}, f32[1,16,2]{1,2,0:T(2,128)}, u32[]{:S(2)}) copy-start(f32[1,16,2]{1,2,0:T(2,128)} %param.17) | copy-start | bytes 388
  219.3 179.6 %all-to-all-start.1 = ((bf16[32,12,7168]{2,1,0:T(8,128)(2,1)}), bf16[32,12,7168]{2,1,0:T(8,128)(2,1)}, u32[]{:S(2)}, u32[]{:S(2)}) async-start(bf16[32,12,7168]{2,1,0:T(8,128)(2,1)} %reshape.205), calls=%async_computation.1 | async-start | bytes 14680064 | tf_op jit(solution)/shard_map/all_to_all | solution.py:101
  226.4 218.3 %all-gather.3.cloned.1.call-start = ((), (), s32[]{:S(2)}) async-start(), calls=%async_computation.4 | async-start | bytes 2703360 | tf_op jit(solution)/shard_map/all_gather | solution.py:136
  227.1 485.7 %all-reduce.2.cloned.1.call-start = ((), (), s32[]{:S(2)}) async-start(), calls=%async_computation.3 | async-start | bytes 8650752 | tf_op jit(solution)/shard_map/psum | solution.py:125
  227.2 176.3 %copy-start.5 = (bf16[1,16,7168]{2,1,0:T(8,128)(2,1)S(1)}, bf16[1,16,7168]{2,1,0:T(8,128)(2,1)}, u32[]{:S(2)}) copy-start(bf16[1,16,7168]{2,1,0:T(8,128)(2,1)} %param.15) | copy-start | bytes 688132
  227.2 184.7 %copy-start.9 = (f32[1,7168]{1,0:T(1,128)S(1)}, f32[1,7168]{1,0:T(1,128)}, u32[]{:S(2)}) copy-start(f32[1,7168]{1,0:T(1,128)} %param.21) | copy-start | bytes 86020
  403.5 34.0 %copy-start.7 = (bf16[1,224,576]{2,1,0:T(8,128)(2,1)S(1)}, bf16[1,224,576]{2,1,0:T(8,128)(2,1)}, u32[]{:S(2)}) copy-start(bf16[1,224,576]{2,1,0:T(8,128)(2,1)} %param.23) | copy-start | bytes 774148
  403.5 34.4 %copy-start.6 = (bf16[1,224,1536]{2,1,0:T(8,128)(2,1)S(1)}, bf16[1,224,1536]{2,1,0:T(8,128)(2,1)}, u32[]{:S(2)}) copy-start(bf16[1,224,1536]{2,1,0:T(8,128)(2,1)} %param.22) | copy-start | bytes 2064388
  404.5 7.2 collective-permute-start
  441.0 1.3 copy-start.3
  441.0 2.7 copy-start.10
  449.0 267.3 %copy-start.4 = (bf16[1,1536,384]{1,2,0:T(8,128)(2,1)S(1)}, bf16[1,1536,384]{1,2,0:T(8,128)(2,1)}, u32[]{:S(2)}) copy-start(bf16[1,1536,384]{1,2,0:T(8,128)(2,1)} %copy.91) | copy-start | bytes 3538948
  716.3 2.8 copy-start.8
  716.4 4.8 copy-start.11
  719.2 3.4 copy-start.2
  738.6 4.0 copy-start.13
  745.9 10.9 %copy-start.1 = (bf16[1,128,7168]{2,1,0:T(8,128)(2,1)S(1)}, bf16[1,128,7168]{2,1,0:T(8,128)(2,1)}, u32[]{:S(2)}) copy-start(bf16[1,128,7168]{2,1,0:T(8,128)(2,1)} %param.20) | copy-start | bytes 5505028
Sparse Core Ops, SparseCore 0:
  230.0 119.6 all-gather.2
  441.2 271.5 all-reduce.1
where the time goes:
time: 765 us; the launch traced here: 764 us
  waiting for transfers between devices  443 us (58%)
  blocking collectives  200 us (26%)
  matrix products  37.1 us (5%)
  local copies, waits for them, and re-layouts  31.7 us (4%)
  other arithmetic  30.6 us (4%)
  between operations  13.8 us (2%)
  starting transfers between devices  7.74 us (1%)
    psum x1, waiting for transfers between devices, per_device(): lax.psum(jnp.concatenate([jnp.dot(columns, down_query, preferred_element_...  264 us
    all_to_all x1, blocking collectives, per_device(): lax.all_to_all(outgoing, 'expert', split_axis=0, concat_axis=0, tiled=True)  175 us
    all_to_all x1, waiting for transfers between devices, per_device(): lax.all_to_all(partial_value.reshape(sources, slot_count, model_width), '...  172 us
    all_to_all x1, blocking collectives, per_device(): lax.all_to_all(normed, 'expert', split_axis=1, concat_axis=0, tiled=True)  24.9 us
  transfers between devices with their start and end apart: 4, of which 3 were waited for; matrix products, arithmetic and copies ran while one was open for 2% of the time, Pallas kernels for 0%

commit v1 on v0

v1 whole, which is shorter than its diff:
```python
import functools

import jax
import jax.numpy as jnp
import numpy as np
from jax import lax
from jax.experimental import pallas as pl
from jax.experimental.pallas import tpu as pltpu
from jax.sharding import PartitionSpec as P

MESH = pl.DeviceIdType.MESH
BF = jnp.bfloat16
F32 = jnp.float32
EPSILON = 1e-06
D = 7168
ROWS = 16
SIDE = 128
WIDE = D + SIDE
HID = 128
QR = 1536
KVR = 512
ROPE = 64
NOPE = 128
KEY = KVR + ROPE
LAT = QR + KEY
LATW = 2176
FB = 224
TOK = 512
CACHE = 2048
PRE = 64
KT = (((1,), (0,)), ((), ()))
NT = (((1,), (1,)), ((), ()))
TN = (((0,), (0,)), ((), ()))


def mm(a, b, dims=KT):
    return lax.dot_general(a, b, dims, preferred_element_type=F32)


class Net:
    def __init__(self, send_sems, recv_sems, places):
        self.send_sems, self.recv_sems, self.places = send_sems, recv_sems, places
        self.ids, self.pending = {}, []

    def copy(self, key, src, dst, place):
        index = self.ids.setdefault(key, len(self.ids))
        return pltpu.make_async_remote_copy(
            src_ref=src,
            dst_ref=dst,
            send_sem=self.send_sems.at[index],
            recv_sem=self.recv_sems.at[index],
            device_id=self.places[place],
            device_id_type=MESH,
        )

    def send(self, key, src, dst, place):
        c = self.copy(key, src, dst, place)
        c.start()
        self.pending.append(c)

    def wait(self, key, ref):
        self.copy(key, ref, ref, "sib").wait_recv()

    def drain(self):
        for c in self.pending:
            c.wait_send()
        self.pending = []


DIRS = (("R", -1), ("L", 1))


def all_gather(n, net, slot, part):
    def pass_on(key, s, what, place):
        net.send(key, part(s, what), part(s, what), place)

    me, mate = slot(0, 0, 0), slot(1, 0, 0)
    pass_on((n, "xA"), me, "A", "xp")
    for way, _ in DIRS:
        pass_on((n, "A", way, 1), me, "A", way)
    pass_on((n, "xB", "", 0), me, "B", "xp")
    for way, _ in DIRS:
        pass_on((n, "B", way, 1), me, "B", way)
    pass_on((n, "s0", "", 0), me, "F", "sib")
    net.wait((n, "xA"), part(mate, "A"))
    for way, _ in DIRS:
        pass_on((n, "A1", way, 1), mate, "A", way)
    net.wait((n, "xB", "", 0), part(mate, "B"))
    pass_on((n, "s1", "", 0), mate, "F", "sib")
    yield 0

    def finish(h):
        if h < 4:
            for way, sign in DIRS:
                s = slot(1, sign * h, 0)
                net.wait((n, "xB", way, h), part(s, "B"))
                pass_on((n, "s1", way, h), s, "F", "sib")
        else:
            s = slot(1, 4, 0)
            net.wait((n, "xB", "R", 4), part(s, "B1"))
            net.wait((n, "xB", "L", 4), part(s, "B2"))
            pass_on((n, "s1", "R", 4), s, "F", "sib")

    for h in range(1, 5):
        for way, sign in DIRS:
            if h < 4 or way == "R":
                s = slot(0, sign * h, 0)
                net.wait((n, "A", way, h), part(s, "A"))
                if h < 3 or (h == 3 and way == "R"):
                    pass_on((n, "A", way, h + 1), s, "A", way)
        for way, sign in DIRS:
            s = slot(0, sign * h, 0)
            half = "B1" if way == "R" else "B2"
            if h < 4:
                net.wait((n, "B", way, h), part(s, "B"))
                pass_on((n, "B", way, h + 1), s, "B" if h < 3 else half, way)
                pass_on((n, "xB", way, h), s, "B", "xp")
                pass_on((n, "s0", way, h), s, "F", "sib")
            else:
                net.wait((n, "B", way, 4), part(s, half))
                pass_on((n, "xB", way, 4), s, half, "xp")
        if h == 4:
            pass_on((n, "s0", "R", 4), slot(0, 4, 0), "F", "sib")
        for way, sign in DIRS:
            if h < 4 or way == "L":
                s = slot(1, sign * h, 0)
                net.wait((n, "A1", way, h), part(s, "A"))
                if h < 3 or (h == 3 and way == "L"):
                    pass_on((n, "A1", way, h + 1), s, "A", way)
        if h >= 2:
            finish(h - 1)
            yield h - 1
    finish(4)
    yield 4


def sib_rows(n, net, slot, part, h):
    slots = []
    for way, sign in DIRS if 0 < h < 4 else (("" if h == 0 else "R", 1),):
        for dx in (0, 1):
            net.wait((n, f"s{dx}", way, h), part(slot(dx, sign * h, 1), "F"))
            slots += [slot(dx, sign * h, 0), slot(dx, sign * h, 1)]
    return slots


def reduce_scatter(n, net, value, cut, ms, mr, xs, xr):
    order = [4, 3, -3, 2, -2, 1, -1, 0]

    def put(key, buf, there, what, val, place):
        cut(buf, what)[...] = val.astype(BF)
        net.send(key, cut(buf, what), cut(there, what), place)

    def got(key, buf, what):
        net.wait(key, cut(buf, what))
        return cut(buf, what)[...].astype(F32)

    def over_x(k):
        put((n, "x", k), xs.at[k], xr.at[k], "B", value(1, order[k], "B"), "xp")

    over_x(0)
    for way, d in (("R", 0), ("L", 1)):
        w = 0 if way == "R" else 1
        put((n, "A", way, 1, d), ms.at[w, 0, d], mr.at[w, 0, d], "A", value(d, 4, "A"), way)
    for k in range(1, 3):
        over_x(k)
    net.wait((n, "x", 0), cut(xr.at[0], "B"))
    for w, (way, half) in enumerate((("R", "B1"), ("L", "B2"))):
        val = value(0, 4, half) + cut(xr.at[0], half)[...].astype(F32)
        put((n, "B", way, 1), ms.at[w, 0, 0], mr.at[w, 0, 0], half, val, way)
    for k in range(3, 8):
        over_x(k)
    yield 1
    for h in range(2, 5):
        for d in (1, 0):
            for w, way in enumerate("RL"):
                dz = (5 - h) * (1 if way == "R" else -1)
                val = value(d, dz, "A")
                if h > 2 or w == d:
                    val = val + got((n, "A", way, h - 1, d), mr.at[w, h - 2, d], "A")
                put((n, "A", way, h, d), ms.at[w, h - 1, d], mr.at[w, h - 1, d], "A", val, way)
        for w, (way, half, rest) in enumerate((("R", "B1", "B2"), ("L", "B2", "B1"))):
            dz = (5 - h) * (1 if way == "R" else -1)
            k = order.index(dz)
            net.wait((n, "x", k), cut(xr.at[k], "B"))
            if h == 2:
                buf = ms.at[w, h - 1, 0]
                val = value(0, dz, rest) + cut(xr.at[k], rest)[...].astype(F32)
                cut(buf, rest)[...] = val.astype(BF)
                val = value(0, dz, half) + cut(xr.at[k], half)[...].astype(F32)
                val = val + got((n, "B", way, 1), mr.at[w, 0, 0], half)
                cut(buf, half)[...] = val.astype(BF)
                net.send((n, "B", way, h), cut(buf, "B"), cut(mr.at[w, h - 1, 0], "B"), way)
            else:
                val = value(0, dz, "B") + cut(xr.at[k], "B")[...].astype(F32)
                val = val + got((n, "B", way, h - 1), mr.at[w, h - 2, 0], "B")
                put((n, "B", way, h), ms.at[w, h - 1, 0], mr.at[w, h - 1, 0], "B", val, way)
        yield h
    val = value(1, 0, "A")
    for w, way in enumerate("RL"):
        val = val + got((n, "A", way, 4, 1), mr.at[w, 3, 1], "A")
    put((n, "xA"), xs.at[7], xr.at[7], "A", val, "xp")
    own = value(0, 0, "A")
    for w, way in enumerate("RL"):
        own = own + got((n, "A", way, 4, 0), mr.at[w, 3, 0], "A")
    val = value(0, 0, "B") + got((n, "x", 7), xr.at[7], "B")
    for w, way in enumerate("RL"):
        val = val + got((n, "B", way, 4), mr.at[w, 3, 0], "B")
    yield "B", val
    yield "A", own + got((n, "xA"), xr.at[7], "A")


def last_cut(ref, a, b):
    return ref.at[..., pl.ds(a, b - a)]


TOK_CUTS = {"A": (0, 3072), "B": (3072, WIDE), "B1": (3072, 5120), "B2": (5120, WIDE), "F": (0, WIDE)}
LAT_CUTS = {"A": (0, 896), "B": (896, LATW), "B1": (896, 1536), "B2": (1536, LATW), "F": (0, LATW)}
PRE_CUTS = {"A": (0, 32), "B": (32, 64), "B1": (32, 48), "B2": (48, 64), "F": (0, 64)}
MIX_CUTS = {"A": (0, 96), "B": (96, 224), "B1": (96, 160), "B2": (160, 224), "F": (0, 224)}


def relay_kernel(
    sections,
    tok_ref, ids_ref, gates_ref, wg_ref, wu_ref, wd_ref, gain_ref, wq_ref, wk_ref, qg_ref, kg_ref, trig_ref, pre_ref,
    lat_out, pre_out,
    buf, wgu, wdn, wt, wdt, hid, hidt, toks_t, ms, mr, xs, xr, arr, sib_arr, arr_s, wqs, wks, lat,
    ms2, mr2, xs2, xr2, send_sems, recv_sems, local_sems,
):
    sec, e = lax.axis_index("section"), lax.axis_index("expert")
    xh, z, c = e // 16, (e // 2) % 8, e % 2

    def at(dx, dz, dc):
        return (xh + dx) % 2 * 16 + (z + dz + 8) % 8 * 2 + (c + dc) % 2

    places = {
        "R": (sec, at(0, 1, 0)),
        "L": (sec, at(0, -1, 0)),
        "xp": (sec, at(1, 0, 0)),
        "sib": (sec, at(0, 0, 1)),
        "next": ((sec + 1) % sections, e),
        "prev": ((sec + sections - 1) % sections, e),
    }
    net = Net(send_sems, recv_sems, places)
    local = []

    def fetch(k, src, dst):
        cp = pltpu.make_async_copy(src, dst, local_sems.at[k])
        cp.start()
        local.append(cp)
        return cp

    def slot(dx, dz, dc):
        return (c + dc) % 2 * 16 + (xh + dx) % 2 * 8 + (z + dz + 8) % 8

    me = slot(0, 0, 0)
    own = fetch(0, tok_ref, buf.at[me, :, pl.ds(0, D)])
    load_g = fetch(1, wg_ref, wgu.at[:, pl.ds(0, HID)])
    load_u = fetch(2, wu_ref, wgu.at[:, pl.ds(HID, HID)])
    load_d = fetch(3, wd_ref, wdn)
    load_q = fetch(4, wq_ref, wqs.at[0])
    load_k = fetch(5, wk_ref, wks.at[0])
    load_p = fetch(6, pre_ref, pre_out.at[e])

    barrier = pltpu.get_barrier_semaphore()
    for there in places.values():
        pl.semaphore_signal(barrier, inc=1, device_id=there, device_id_type=MESH)

    lane = lax.broadcasted_iota(jnp.int32, (ROWS, SIDE), 1)
    g = jnp.zeros((ROWS, SIDE), F32)
    for k in range(2):
        g = g + jnp.where(ids_ref[:, k : k + 1] == lane % 4, gates_ref[:, k : k + 1], 0.0)
    high = g.astype(BF)
    low = (g - high.astype(F32)).astype(BF)
    side = jnp.where(lane < 4, high.astype(F32), jnp.where(lane < 8, low.astype(F32), 0.0)).astype(BF)
    buf[me, :, D:WIDE] = side
    pl.semaphore_wait(barrier, len(places))
    own.wait()

    def tok_part(s, what):
        return last_cut(buf.at[s], *TOK_CUTS[what])

    expert = e // 8
    gather = all_gather("t", net, slot, tok_part)
    next(gather)
    load_q.wait()
    net.send("wq", wqs.at[0], wqs.at[1], "sib")
    load_k.wait()
    net.send("wk", wks.at[0], wks.at[1], "sib")

    load_d.wait()
    for k in range(8):
        wt[4 * k : 4 * k + 4] = wdn[:, 896 * k : 896 * (k + 1)].T.reshape(4, FB, HID)
    half = pl.ds(pl.multiple_of(c * HID, HID), HID)
    pairs = wt.reshape(16, 2, FB, HID)
    net.send("wd", pairs.at[:, (c + 1) % 2], wdt.at[:, :, half], "sib")
    keep_d = fetch(7, pairs.at[:, c], wdt.at[:, :, half])

    load_g.wait()
    load_u.wait()

    def experts(h):
        slots = sib_rows("t", net, slot, tok_part, h)
        m = len(slots) * ROWS
        acc = jnp.zeros((m, 2 * HID), F32)
        for k in range(7):
            rows = jnp.concatenate([buf[s, :, 1024 * k : 1024 * (k + 1)] for s in slots], axis=0)
            acc = acc + mm(rows, wgu[1024 * k : 1024 * (k + 1), :])
        side = jnp.concatenate([buf[s, :, D:WIDE] for s in slots], axis=0).astype(F32)
        lane = lax.broadcasted_iota(jnp.int32, (m, SIDE), 1)
        gate = jnp.sum(jnp.where((lane % 4 == expert) & (lane < 8), side, 0.0), axis=1, keepdims=True)
        gp, up = acc[:, :HID], acc[:, HID:]
        val = (gp / (1.0 + jnp.exp(-gp)) * up * gate).astype(BF)
        for i, s in enumerate(slots):
            hid[pl.ds(pl.multiple_of(s * ROWS, ROWS), ROWS), half] = val[ROWS * i : ROWS * (i + 1)]

    experts(0)
    for h in gather:
        experts(h)
    net.send("hid", hid.at[:, half], hid.at[:, half], "sib")

    start = jnp.minimum(FB * e // 128 * 128, D - 384)
    window = buf[:, :, pl.ds(pl.multiple_of(start, 128), 384)].reshape(TOK, 384)
    toks_t[...] = window.T

    other = pl.ds(pl.multiple_of((c + 1) % 2 * HID, HID), HID)
    net.wait("hid", hid.at[:, other])
    net.wait("wd", wdt.at[:, :, other])
    keep_d.wait()
    hidt[...] = hid[...].T

    def mixed_term(dx, dz, what):
        a, b = MIX_CUTS[what]
        block = (xh + dx) % 2 * 8 + (z + dz + 8) % 8
        return mm(wdt[block, a:b, :], hidt[...])

    def mix_cut(ref, what):
        a, b = MIX_CUTS[what]
        return ref.at[pl.ds(a, b - a)]

    load_p.wait()
    off = FB * e - start
    for got in reduce_scatter("m", net, mixed_term, mix_cut, ms, mr, xs, xr):
        if not isinstance(got, tuple):
            continue
        what, val = got
        a, b = MIX_CUTS[what]
        rows = toks_t[pl.ds(pl.multiple_of(off + a, 32), b - a), :].astype(F32)
        arr_s[a:b] = (val + rows).astype(BF)
        net.send(("next", what), arr_s.at[pl.ds(a, b - a)], arr.at[pl.ds(a, b - a)], "next")

    def pre_part(s, what):
        a, b = PRE_CUTS[what]
        return pre_out.at[s, pl.ds(a, b - a)]

    prefix = all_gather("p", net, at, pre_part)
    next(prefix)

    for what in "BA":
        net.wait(("next", what), mix_cut(arr, what))
    mine = pl.ds(pl.multiple_of(c * 256, 256), 256)
    theirs = pl.ds(pl.multiple_of((c + 1) % 2 * 256, 256), 256)
    net.send("arr", arr.at[:, theirs], sib_arr, "sib")
    net.wait("wq", wqs.at[1])
    net.wait("wk", wks.at[1])
    squares = jnp.zeros((1, 256), F32)
    for i in range(2):
        if i == 1:
            net.wait("arr", sib_arr)
        x = (arr[:, mine] if i == 0 else sib_arr[...]).astype(F32)
        squares = squares + jnp.sum(x * x, axis=0, keepdims=True)
        scaled = (x * gain_ref[i, :, 0:1]).T.astype(BF)
        if i == 0:
            lat[:, 0:QR] = mm(scaled, wqs[0])
            lat[:, QR:LAT] = mm(scaled, wks[0])
        else:
            lat[:, 0:QR] += mm(scaled, wqs[1])
            lat[:, QR:LAT] += mm(scaled, wks[1])
    lat[:, LAT:LATW] = jnp.broadcast_to(squares, (128, 256)).T[:, 0 : LATW - LAT]

    def lat_term(dx, dz, what):
        a, b = LAT_CUTS[what]
        block = (xh + dx) % 2 * 8 + (z + dz + 8) % 8
        return lat[pl.ds(pl.multiple_of(block * ROWS, ROWS), ROWS), a:b]

    def lat_cut(ref, what):
        return last_cut(ref, *LAT_CUTS[what])

    sums = {}
    for got in reduce_scatter("l", net, lat_term, lat_cut, ms2, mr2, xs2, xr2):
        if isinstance(got, tuple):
            sums[got[0]] = got[1]
        else:
            next(prefix, None)
    total = jnp.concatenate([sums["A"], sums["B"]], axis=1)
    scale = lax.rsqrt(total[:, LAT : LAT + 1] * (1.0 / D) + EPSILON)

    def rms(v, gain):
        v = v * scale
        return (v * lax.rsqrt(jnp.mean(v * v, axis=1, keepdims=True) + EPSILON) * gain).astype(BF)

    lat_out[e, :, 0:QR] = rms(total[:, 0:QR], qg_ref[...])
    lat_out[e, :, QR : QR + KVR] = rms(total[:, QR : QR + KVR], kg_ref[...])
    tail = total[:, QR + KVR :] * scale
    first, second = tail[:, 0:32], tail[:, 32:64]
    cos, sin = trig_ref[e, :, 0:32], trig_ref[e, :, 32:64]
    turned = jnp.concatenate([first * cos - second * sin, first * sin + second * cos], axis=1)
    lat_out[e, :, QR + KVR : LAT] = turned.astype(BF)
    lat_out[e, :, LAT:LATW] = jnp.zeros((ROWS, LATW - LAT), BF)

    def lat_part(s, what):
        return last_cut(lat_out.at[s], *LAT_CUTS[what])

    for _ in prefix:
        pass
    for h in range(5):
        sib_rows("p", net, at, pre_part, h)
    for h in all_gather("o", net, at, lat_part):
        sib_rows("o", net, at, lat_part, h)
    net.drain()


def trig_table():
    half = ROPE // 2
    frequency = 10000.0 ** (-np.arange(half) / half)
    angles = (CACHE + np.arange(TOK))[:, None] * frequency[None, :].astype(np.float32)
    angles = angles.astype(np.float32).astype(np.float64)
    both = np.concatenate([np.cos(angles), np.sin(angles)], axis=1)
    return both.astype(np.float32)


def attend_kernel(lat_ref, pre_ref, trig_ref, wuq_ref, wuk_ref, wuv_ref, out_ref, kv, qs, acc_ref, m_ref, l_ref):
    scale = (NOPE + ROPE) ** (-0.5)
    trig = trig_ref[...]
    cos, sin = trig[:, 0:32], trig[:, 32:64]
    kv[:, 0:KEY] = lat_ref[:, QR:LAT]
    q = mm(lat_ref[:, 0:QR], wuq_ref[...])
    for h in range(2):
        base = h * (NOPE + ROPE)
        nope = q[:, base : base + NOPE].astype(BF)
        qs[h, :, 0:KVR] = mm(nope, wuk_ref[h]).astype(BF)
        first = q[:, base + NOPE : base + NOPE + 32]
        second = q[:, base + NOPE + 32 : base + NOPE + 64]
        turned = jnp.concatenate([first * cos - second * sin, first * sin + second * cos], axis=1)
        qs[h, :, KVR:KEY] = turned.astype(BF)
    for h in range(2):
        for i in range(2):
            rows = pl.ds(256 * i, 256)
            query = qs[h, rows, :]
            for b in range(5):
                if b < 4:
                    keys = pre_ref[512 * b : 512 * (b + 1), :]
                else:
                    keys = kv[...]
                s = mm(query, keys, NT) * scale
                if b == 4:
                    t = lax.broadcasted_iota(jnp.int32, s.shape, 0) + 256 * i
                    j = lax.broadcasted_iota(jnp.int32, s.shape, 1)
                    s = jnp.where(j <= t, s, -jnp.inf)
                top = jnp.max(s, axis=1, keepdims=True)
                if b == 0:
                    m = top
                    p = jnp.exp(s - m)
                    l = jnp.sum(p, axis=1, keepdims=True)
                    acc = mm(p.astype(BF), keys[:, 0:KVR])
                else:
                    new = jnp.maximum(m, top)
                    fade = jnp.exp(m - new)
                    p = jnp.exp(s - new)
                    l = l * fade + jnp.sum(p, axis=1, keepdims=True)
                    acc = acc * fade + mm(p.astype(BF), keys[:, 0:KVR])
                    m = new
            latent = (acc / l).astype(BF)
            out_ref[rows, 128 * h : 128 * (h + 1)] = mm(latent, wuv_ref[h]).astype(BF)


def per_device(
    sections, tokens, expert_ids, gate_values, w_gate, w_up, w_down, norm_gain, w_dq, w_dkv, q_gain, kv_gain, w_uq, w_uk,
    w_uv, prefix_cache,
):
    e = lax.axis_index("expert")
    gains = norm_gain[0].reshape(32, FB)
    pair = jnp.stack([lax.dynamic_index_in_dim(gains, k, 0, False) for k in (e, e // 2 * 2 + 1 - e % 2)])
    pair = jnp.broadcast_to(pair[:, :, None], (2, FB, 128))
    table = trig_table()
    vm = pl.BlockSpec(memory_space=pltpu.VMEM)
    anyw = pl.BlockSpec(memory_space=pl.ANY)
    V = pltpu.VMEM
    lat_rows, prefix = pl.pallas_call(
        functools.partial(relay_kernel, sections),
        name="relay",
        out_shape=(jax.ShapeDtypeStruct((32, ROWS, LATW), BF), jax.ShapeDtypeStruct((32, PRE, KEY), BF)),
        in_specs=[anyw, vm, vm, anyw, anyw, anyw, vm, anyw, anyw, vm, vm, vm, anyw],
        out_specs=(vm, vm),
        scratch_shapes=[
            V((32, ROWS, WIDE), BF),
            V((D, 2 * HID), BF),
            V((HID, D), BF),
            V((32, FB, HID), BF),
            V((16, FB, 2 * HID), BF),
            V((TOK, 2 * HID), BF),
            V((2 * HID, TOK), BF),
            V((384, TOK), BF),
            V((2, 4, 2, FB, TOK), BF),
            V((2, 4, 2, FB, TOK), BF),
            V((8, FB, TOK), BF),
            V((8, FB, TOK), BF),
            V((FB, TOK), BF),
            V((FB, TOK // 2), BF),
            V((FB, TOK), BF),
            V((2, FB, QR), BF),
            V((2, FB, KEY), BF),
            V((TOK // 2, LATW), F32),
            V((2, 4, 2, ROWS, LATW), BF),
            V((2, 4, 2, ROWS, LATW), BF),
            V((8, ROWS, LATW), BF),
            V((8, ROWS, LATW), BF),
            pltpu.SemaphoreType.DMA((256,)),
            pltpu.SemaphoreType.DMA((256,)),
            pltpu.SemaphoreType.DMA((8,)),
        ],
        compiler_params=pltpu.CompilerParams(collective_id=0, has_side_effects=True, vmem_limit_bytes=58 << 20),
        cost_estimate=pl.CostEstimate(flops=4 * 10**9, bytes_accessed=12 * 10**6, transcendentals=10**6),
    )(
        tokens[0], expert_ids[0], gate_values[0], w_gate[0], w_up[0], w_down[0], pair, w_dq[0], w_dkv[0], q_gain,
        kv_gain, jnp.asarray(table.reshape(32, ROWS, ROPE)), prefix_cache[0],
    )
    out = pl.pallas_call(
        attend_kernel,
        name="attend",
        out_shape=jax.ShapeDtypeStruct((TOK, 256), BF),
        in_specs=[vm] * 6,
        out_specs=vm,
        scratch_shapes=[
            V((TOK, KEY), BF),
            V((2, TOK, KEY), BF),
            V((8, 128), F32),
            V((8, 128), F32),
            V((8, 128), F32),
        ],
        compiler_params=pltpu.CompilerParams(vmem_limit_bytes=58 << 20),
        cost_estimate=pl.CostEstimate(flops=9 * 10**9, bytes_accessed=8 * 10**6, transcendentals=3 * 10**6),
    )(
        lat_rows.reshape(TOK, LATW), prefix.reshape(CACHE, KEY), jnp.asarray(table), w_uq[0], w_uk[0], w_uv[0]
    )
    return out[None]


def solution(mesh):
    placed = (
        P("section", "expert", None),
        P("section", "expert", None),
        P("section", "expert", None),
        P("section", None, "expert"),
        P("section", None, "expert"),
        P("section", "expert", None),
        P("section", None),
        P("section", "expert", None),
        P("section", "expert", None),
        P("section", None),
        P("section", None),
        P("section", None, "expert"),
        P("section", "expert", None, None),
        P("section", "expert", None, None),
        P("section", "expert", None),
    )
    return jax.shard_map(
        functools.partial(per_device, mesh.shape["section"]),
        mesh=mesh,
        in_specs=placed,
        out_specs=P("section", None, "expert"),
        check_vma=False,
    )
```

time: 765 us -> 168 us (0.22)
  waiting for transfers between devices: 443 us -> 0 us
  blocking collectives: 200 us -> 0 us
  Pallas kernels: 0 us -> 162 us
  matrix products: 37.1 us -> 0 us
  other arithmetic: 30.6 us -> 1.47 us
  local copies, waits for them, and re-layouts: 31.7 us -> 4.11 us
  between operations: 13.8 us -> 0.03 us
  starting transfers between devices: 7.74 us -> 0 us
    psum x1 -> x0, waiting for transfers between devices: 264 us -> none  [per_device(): lax.psum(jnp.concatenate([jnp.dot(columns, down_query, preferred_element_...]
    all_to_all x2 -> x0, blocking collectives: 200 us -> none  [the longest x1 175 us: per_device(): lax.all_to_all(outgoing, 'expert', split_axis=0, concat_axis=0, tiled=True)]
    all_to_all x1 -> x0, waiting for transfers between devices: 172 us -> none  [per_device(): lax.all_to_all(partial_value.reshape(sources, slot_count, model_width), '...]
    pallas_call x0 -> x2, Pallas kernels: none -> 162 us  [the longest x1 146 us: per_device(): pl.pallas_call(functools.partial(relay_kernel, sections), name='relay', o...]
    dot_general x10 -> x0, matrix products: 37.1 us -> none  [the longest x1 11.5 us: per_device(): jnp.dot(hidden, hidden_down, preferred_element_type=jnp.float32)]
    reshape x2 -> x0, local copies, waits for them, and re-layouts: 16.3 us -> none  [the longest x1 8.25 us: per_device(): flat_rows = slot_rows.reshape(sources * slot_count, model_width)]
    concatenate x2 -> x0, other arithmetic: 14.2 us -> none  [the longest x1 11.7 us: per_device(): key_rows = jnp.concatenate([cached, latent_rows[:, query_width:]], axis=0)]
    reduce_sum x6 -> x0, other arithmetic: 8.3 us -> none  [the longest x1 4.55 us: per_device(): jnp.sum(returned.reshape(EXPERTS, group_size, capacity, model_width).asty...]
  transfers between devices with their start and end apart: 4 -> 0, of which waited for: 3 -> 0; matrix products, arithmetic and copies ran while one was open for 2% -> 0% of each run, Pallas kernels for 0% -> 0%
where the time goes in v1:
time: 168 us
  Pallas kernels  162 us (96%)
  local copies, waits for them, and re-layouts  4.11 us (2%)
    pallas_call x1, Pallas kernels, per_device(): pl.pallas_call(functools.partial(relay_kernel, sections), name='relay', o...  146 us
    pallas_call x1, Pallas kernels, per_device(): pl.pallas_call(attend_kernel, name='attend', out_shape=jax.ShapeDtypeStru...  16.2 us

profile of v1, /device:TPU:1, one launch (start us, length us, event | category | flops | bytes accessed | tf_op | source)
XLA Modules:
  0.0 167.9 jit_solution(16494367341599058016)
XLA Ops:
  0.0 1.3 copy.18.ids_ref
  1.4 1.3 copy.19.gates_ref
  2.7 0.5 broadcast.6
  3.2 1.5 reduce.3
  4.7 0.1 reshape_squeeze.3
  4.8 0.8 broadcast_in_dim.4.gain_ref
  5.6 146.1 %relay.1 = (bf16[32,16,2176]{2,1,0:T(8,128)(2,1)}, bf16[32,64,576]{2,1,0:T(8,128)(2,1)}) custom-call(bf16[16,7168]{1,0:T(8,128)(2,1)} %bitcast.25, s32[16,2]{1,0:T(8,128)} %copy.18.ids_ref, f32[16,2]{1,0:T(8,128)} %copy.19.gates_ref, bf16[7168,128]{1,0:T(8,128)(2,1)} %bitcast.17, bf16[7168,128]{1,0:T(8,128)(2,1)} %bitcast.18, bf16[128,7168]{1,0:T(8,128)(2,1)} %bitcast.19, ...), custom_call_target="tpu_custom_call" | custom-call | flops 4000000000 | bytes 12000000 | tf_op jit(solution)/shard_map/relay/pallas_call | solution.py:488
  151.7 16.2 %attend.1 = bf16[512,256]{1,0:T(8,128)(2,1)} custom-call(bf16[512,2176]{1,0:T(8,128)(2,1)} %bitcast.28, bf16[2048,576]{1,0:T(8,128)(2,1)} %bitcast.27, f32[512,64]{1,0:T(8,128)} %constant.41.clone.trig_ref, bf16[1536,384]{1,0:T(8,128)(2,1)} %bitcast.20, bf16[2,128,512]{2,1,0:T(8,128)(2,1)} %bitcast.23, bf16[2,512,128]{2,1,0:T(8,128)(2,1)} %bitcast.24), custom_call_target="tpu_custom_call" | custom-call | flops 8999999488 | bytes 8000000 | tf_op jit(solution)/shard_map/attend/pallas_call | solution.py:527
  (2 shorter events, 0.0 us)

commit v2 on v1

--- a/solution.py
+++ b/solution.py
@@ -82,12 +82,13 @@
     for way, _ in DIRS:
         pass_on((n, "B", way, 1), me, "B", way)
     pass_on((n, "s0", "", 0), me, "F", "sib")
+    yield None
     net.wait((n, "xA"), part(mate, "A"))
     for way, _ in DIRS:
         pass_on((n, "A1", way, 1), mate, "A", way)
+    yield None
     net.wait((n, "xB", "", 0), part(mate, "B"))
     pass_on((n, "s1", "", 0), mate, "F", "sib")
-    yield 0
 
     def finish(h):
         if h < 4:
@@ -108,6 +109,9 @@
                 net.wait((n, "A", way, h), part(s, "A"))
                 if h < 3 or (h == 3 and way == "R"):
                     pass_on((n, "A", way, h + 1), s, "A", way)
+        yield None
+        if h >= 2:
+            finish(h - 1)
         for way, sign in DIRS:
             s = slot(0, sign * h, 0)
             half = "B1" if way == "R" else "B2"
@@ -121,15 +125,14 @@
                 pass_on((n, "xB", way, 4), s, half, "xp")
         if h == 4:
             pass_on((n, "s0", "R", 4), slot(0, 4, 0), "F", "sib")
+        yield h - 1
         for way, sign in DIRS:
             if h < 4 or way == "L":
                 s = slot(1, sign * h, 0)
                 net.wait((n, "A1", way, h), part(s, "A"))
                 if h < 3 or (h == 3 and way == "L"):
                     pass_on((n, "A1", way, h + 1), s, "A", way)
-        if h >= 2:
-            finish(h - 1)
-            yield h - 1
+        yield None
     finish(4)
     yield 4
 
@@ -155,58 +158,70 @@
         return cut(buf, what)[...].astype(F32)
 
     def over_x(k):
-        put((n, "x", k), xs.at[k], xr.at[k], "B", value(1, order[k], "B"), "xp")
-
-    over_x(0)
-    for way, d in (("R", 0), ("L", 1)):
-        w = 0 if way == "R" else 1
-        put((n, "A", way, 1, d), ms.at[w, 0, d], mr.at[w, 0, d], "A", value(d, 4, "A"), way)
-    for k in range(1, 3):
-        over_x(k)
-    net.wait((n, "x", 0), cut(xr.at[0], "B"))
-    for w, (way, half) in enumerate((("R", "B1"), ("L", "B2"))):
-        val = value(0, 4, half) + cut(xr.at[0], half)[...].astype(F32)
-        put((n, "B", way, 1), ms.at[w, 0, 0], mr.at[w, 0, 0], half, val, way)
-    for k in range(3, 8):
-        over_x(k)
-    yield 1
-    for h in range(2, 5):
+        if k < 8:
+            put((n, "x", k), xs.at[k], xr.at[k], "B", value(1, order[k], "B"), "xp")
+
+    def from_x(k):
+        net.wait((n, "x", k), cut(xr.at[k], "B"))
+        over_x(k + 3)
+
+    def hop_a(h):
         for d in (1, 0):
             for w, way in enumerate("RL"):
-                dz = (5 - h) * (1 if way == "R" else -1)
-                val = value(d, dz, "A")
-                if h > 2 or w == d:
+                if h == 1 and w != d:
+                    continue
+                val = value(d, (5 - h) * (1 if way == "R" else -1), "A")
+                if h > 2 or (h == 2 and w == d):
                     val = val + got((n, "A", way, h - 1, d), mr.at[w, h - 2, d], "A")
                 put((n, "A", way, h, d), ms.at[w, h - 1, d], mr.at[w, h - 1, d], "A", val, way)
+
+    def hop_b(h):
         for w, (way, half, rest) in enumerate((("R", "B1", "B2"), ("L", "B2", "B1"))):
             dz = (5 - h) * (1 if way == "R" else -1)
-            k = order.index(dz)
-            net.wait((n, "x", k), cut(xr.at[k], "B"))
-            if h == 2:
-                buf = ms.at[w, h - 1, 0]
+            k = order.index(dz if h > 1 else 4)
+            if h > 1 or w == 0:
+                from_x(k)
+            buf, there = ms.at[w, h - 1, 0], mr.at[w, h - 1, 0]
+            if h == 1:
+                val = value(0, 4, half) + cut(xr.at[k], half)[...].astype(F32)
+                put((n, "B", way, 1), buf, there, half, val, way)
+            elif h == 2:
                 val = value(0, dz, rest) + cut(xr.at[k], rest)[...].astype(F32)
                 cut(buf, rest)[...] = val.astype(BF)
                 val = value(0, dz, half) + cut(xr.at[k], half)[...].astype(F32)
                 val = val + got((n, "B", way, 1), mr.at[w, 0, 0], half)
                 cut(buf, half)[...] = val.astype(BF)
-                net.send((n, "B", way, h), cut(buf, "B"), cut(mr.at[w, h - 1, 0], "B"), way)
+                net.send((n, "B", way, h), cut(buf, "B"), cut(there, "B"), way)
             else:
                 val = value(0, dz, "B") + cut(xr.at[k], "B")[...].astype(F32)
                 val = val + got((n, "B", way, h - 1), mr.at[w, h - 2, 0], "B")
-                put((n, "B", way, h), ms.at[w, h - 1, 0], mr.at[w, h - 1, 0], "B", val, way)
+                put((n, "B", way, h), buf, there, "B", val, way)
+
+    over_x(0)
+    hop_a(1)
+    over_x(1)
+    over_x(2)
+    yield 1
+    for h in range(2, 5):
+        hop_a(h)
+        hop_b(h - 1)
         yield h
     val = value(1, 0, "A")
     for w, way in enumerate("RL"):
         val = val + got((n, "A", way, 4, 1), mr.at[w, 3, 1], "A")
     put((n, "xA"), xs.at[7], xr.at[7], "A", val, "xp")
+    hop_b(4)
+    yield 5
     own = value(0, 0, "A")
     for w, way in enumerate("RL"):
         own = own + got((n, "A", way, 4, 0), mr.at[w, 3, 0], "A")
-    val = value(0, 0, "B") + got((n, "x", 7), xr.at[7], "B")
+    yield "A", own + got((n, "xA"), xr.at[7], "A")
+    val = value(0, 0, "B")
+    from_x(7)
+    val = val + cut(xr.at[7], "B")[...].astype(F32)
     for w, way in enumerate("RL"):
         val = val + got((n, "B", way, 4), mr.at[w, 3, 0], "B")
     yield "B", val
-    yield "A", own + got((n, "xA"), xr.at[7], "A")
 
 
 def last_cut(ref, a, b):
@@ -216,15 +231,16 @@
 TOK_CUTS = {"A": (0, 3072), "B": (3072, WIDE), "B1": (3072, 5120), "B2": (5120, WIDE), "F": (0, WIDE)}
 LAT_CUTS = {"A": (0, 896), "B": (896, LATW), "B1": (896, 1536), "B2": (1536, LATW), "F": (0, LATW)}
 PRE_CUTS = {"A": (0, 32), "B": (32, 64), "B1": (32, 48), "B2": (48, 64), "F": (0, 64)}
-MIX_CUTS = {"A": (0, 96), "B": (96, 224), "B1": (96, 160), "B2": (160, 224), "F": (0, 224)}
+MIX_CUTS = {"A": (0, 112), "B": (112, 224), "B1": (112, 176), "B2": (176, 224), "F": (0, 224)}
 
 
 def relay_kernel(
     sections,
     tok_ref, ids_ref, gates_ref, wg_ref, wu_ref, wd_ref, gain_ref, wq_ref, wk_ref, qg_ref, kg_ref, trig_ref, pre_ref,
-    lat_out, pre_out,
+    wuq_ref, wuk_ref, wuv_ref,
+    out_ref,
     buf, wgu, wdn, wt, wdt, hid, hidt, toks_t, ms, mr, xs, xr, arr, sib_arr, arr_s, wqs, wks, lat,
-    ms2, mr2, xs2, xr2, send_sems, recv_sems, local_sems,
+    ms2, mr2, xs2, xr2, lat_out, pre_out, gcol, wuq, wuk, wuv, qs, acc_s, max_s, sum_s, send_sems, recv_sems, local_sems,
 ):
     sec, e = lax.axis_index("section"), lax.axis_index("expert")
     xh, z, c = e // 16, (e // 2) % 8, e % 2
@@ -260,19 +276,37 @@
     load_q = fetch(4, wq_ref, wqs.at[0])
     load_k = fetch(5, wk_ref, wks.at[0])
     load_p = fetch(6, pre_ref, pre_out.at[e])
+    load_uq = fetch(8, wuq_ref, wuq)
+    load_uk = fetch(9, wuk_ref, wuk)
+    load_uv = fetch(10, wuv_ref, wuv)
 
     barrier = pltpu.get_barrier_semaphore()
     for there in places.values():
         pl.semaphore_signal(barrier, inc=1, device_id=there, device_id_type=MESH)
 
     lane = lax.broadcasted_iota(jnp.int32, (ROWS, SIDE), 1)
+    diag = lax.broadcasted_iota(jnp.int32, (ROWS, ROWS), 0) == lax.broadcasted_iota(jnp.int32, (ROWS, ROWS), 1)
     g = jnp.zeros((ROWS, SIDE), F32)
     for k in range(2):
-        g = g + jnp.where(ids_ref[:, k : k + 1] == lane % 4, gates_ref[:, k : k + 1], 0.0)
+        chosen = jnp.sum(jnp.where(diag, ids_ref[k : k + 1, :], 0), axis=1, keepdims=True)
+        weight = jnp.sum(jnp.where(diag, gates_ref[k : k + 1, :], 0.0), axis=1, keepdims=True)
+        g = g + jnp.where(chosen == lane % 4, weight, 0.0)
     high = g.astype(BF)
     low = (g - high.astype(F32)).astype(BF)
     side = jnp.where(lane < 4, high.astype(F32), jnp.where(lane < 8, low.astype(F32), 0.0)).astype(BF)
     buf[me, :, D:WIDE] = side
+
+    load_d.wait()
+    for k in range(8):
+        wt[4 * k : 4 * k + 4] = wdn[:, 896 * k : 896 * (k + 1)].T.reshape(4, FB, HID)
+
+    def window(owner):
+        return jnp.minimum(FB * owner // 128 * 128, D - 384)
+
+    for i in range(2):
+        first = window(at(0, 0, i))
+        piece = gain_ref[0:1, pl.ds(pl.multiple_of(first, 128), 384)]
+        gcol[i] = jnp.broadcast_to(piece, (128, 384)).T
     pl.semaphore_wait(barrier, len(places))
     own.wait()
 
@@ -287,9 +321,6 @@
     load_k.wait()
     net.send("wk", wks.at[0], wks.at[1], "sib")
 
-    load_d.wait()
-    for k in range(8):
-        wt[4 * k : 4 * k + 4] = wdn[:, 896 * k : 896 * (k + 1)].T.reshape(4, FB, HID)
     half = pl.ds(pl.multiple_of(c * HID, HID), HID)
     pairs = wt.reshape(16, 2, FB, HID)
     net.send("wd", pairs.at[:, (c + 1) % 2], wdt.at[:, :, half], "sib")
@@ -313,14 +344,26 @@
         for i, s in enumerate(slots):
             hid[pl.ds(pl.multiple_of(s * ROWS, ROWS), ROWS), half] = val[ROWS * i : ROWS * (i + 1)]
 
-    experts(0)
+    def pre_part(s, what):
+        a, b = PRE_CUTS[what]
+        return pre_out.at[s, pl.ds(a, b - a)]
+
+    prefix = all_gather("p", net, at, pre_part)
+
+    def ticks(count):
+        for _ in range(count):
+            next(prefix, None)
+
     for h in gather:
-        experts(h)
+        if h is not None:
+            if h == 4:
+                load_p.wait()
+                ticks(1)
+            experts(h)
     net.send("hid", hid.at[:, half], hid.at[:, half], "sib")
 
-    start = jnp.minimum(FB * e // 128 * 128, D - 384)
-    window = buf[:, :, pl.ds(pl.multiple_of(start, 128), 384)].reshape(TOK, 384)
-    toks_t[...] = window.T
+    start = window(e)
+    toks_t[...] = buf[:, :, pl.ds(pl.multiple_of(start, 128), 384)].reshape(TOK, 384).T
 
     other = pl.ds(pl.multiple_of((c + 1) % 2 * HID, HID), HID)
     net.wait("hid", hid.at[:, other])
@@ -337,25 +380,19 @@
         a, b = MIX_CUTS[what]
         return ref.at[pl.ds(a, b - a)]
 
-    load_p.wait()
     off = FB * e - start
     for got in reduce_scatter("m", net, mixed_term, mix_cut, ms, mr, xs, xr):
         if not isinstance(got, tuple):
+            ticks({1: 1, 5: 2}.get(got, 0))
             continue
         what, val = got
         a, b = MIX_CUTS[what]
-        rows = toks_t[pl.ds(pl.multiple_of(off + a, 32), b - a), :].astype(F32)
+        rows = toks_t[pl.ds(pl.multiple_of(off + a, 16), b - a), :].astype(F32)
         arr_s[a:b] = (val + rows).astype(BF)
         net.send(("next", what), arr_s.at[pl.ds(a, b - a)], arr.at[pl.ds(a, b - a)], "next")
-
-    def pre_part(s, what):
-        a, b = PRE_CUTS[what]
-        return pre_out.at[s, pl.ds(a, b - a)]
-
-    prefix = all_gather("p", net, at, pre_part)
-    next(prefix)
-
-    for what in "BA":
+    ticks(4)
+
+    for what in "AB":
         net.wait(("next", what), mix_cut(arr, what))
     mine = pl.ds(pl.multiple_of(c * 256, 256), 256)
     theirs = pl.ds(pl.multiple_of((c + 1) % 2 * 256, 256), 256)
@@ -368,7 +405,8 @@
             net.wait("arr", sib_arr)
         x = (arr[:, mine] if i == 0 else sib_arr[...]).astype(F32)
         squares = squares + jnp.sum(x * x, axis=0, keepdims=True)
-        scaled = (x * gain_ref[i, :, 0:1]).T.astype(BF)
+        shift = FB * at(0, 0, i) - window(at(0, 0, i))
+        scaled = (x * gcol[i, pl.ds(pl.multiple_of(shift, 32), FB), 0:1]).T.astype(BF)
         if i == 0:
             lat[:, 0:QR] = mm(scaled, wqs[0])
             lat[:, QR:LAT] = mm(scaled, wks[0])
@@ -390,7 +428,7 @@
         if isinstance(got, tuple):
             sums[got[0]] = got[1]
         else:
-            next(prefix, None)
+            ticks(2)
     total = jnp.concatenate([sums["A"], sums["B"]], axis=1)
     scale = lax.rsqrt(total[:, LAT : LAT + 1] * (1.0 / D) + EPSILON)
 
@@ -410,13 +448,78 @@
     def lat_part(s, what):
         return last_cut(lat_out.at[s], *LAT_CUTS[what])
 
+    for cp in (load_uq, load_uk, load_uv):
+        cp.wait()
+    groups = {}
+
+    def queries(h):
+        slots = sib_rows("o", net, at, lat_part, h)
+        m = len(slots) * ROWS
+        base = {0: 0, 1: 128, 2: 384, 3: 640, 4: 896}[h]
+        rows = jnp.concatenate([lat_out[s, :, 0:QR] for s in slots], axis=0)
+        turn = jnp.concatenate([trig_ref[s] for s in slots], axis=0)
+        cos, sin = turn[:, 0:32], turn[:, 32:64]
+        q = mm(rows, wuq[...])
+        for k in range(2):
+            a, own_rows = k * (NOPE + ROPE), slice(base + k * m, base + (k + 1) * m)
+            qs[own_rows, 0:KVR] = mm(q[:, a : a + NOPE].astype(BF), wuk[k]).astype(BF)
+            first, second = q[:, a + NOPE : a + NOPE + 32], q[:, a + NOPE + 32 : a + NOPE + 64]
+            turned = jnp.concatenate([first * cos - second * sin, first * sin + second * cos], axis=1)
+            qs[own_rows, KVR:KEY] = turned.astype(BF)
+        query = qs[base : base + 2 * m, :]
+        score, top = [], None
+        for b in range(4):
+            keys = pre_out[8 * b : 8 * b + 8].reshape(512, KEY)
+            score.append(mm(query, keys, NT))
+            high = jnp.max(score[-1], axis=1, keepdims=True)
+            top = high if top is None else jnp.maximum(top, high)
+        total, mixed = 0.0, 0.0
+        for b in range(4):
+            keys = pre_out[8 * b : 8 * b + 8, :, 0:KVR].reshape(512, KVR)
+            p = jnp.exp2(score[b] * SHARP - top * SHARP)
+            total = total + jnp.sum(p, axis=1, keepdims=True)
+            mixed = mixed + mm(p.astype(BF), keys)
+        acc_s[base : base + 2 * m, :] = mixed
+        max_s[base : base + 2 * m, :] = jnp.broadcast_to(top, (2 * m, 128))
+        sum_s[base : base + 2 * m, :] = jnp.broadcast_to(total, (2 * m, 128))
+        groups[h] = (base, m, slots)
+
+    def new_keys(h):
+        base, m, slots = groups[h]
+        both = slice(base, base + 2 * m)
+        keys = lat_out[:, :, QR:LAT].reshape(TOK, KEY)
+        row = lax.broadcasted_iota(jnp.int32, (ROWS, 1), 0)
+        when = jnp.concatenate([row + s * ROWS for s in slots] * 2, axis=0)
+        score = mm(qs[both, :], keys, NT)
+        score = jnp.where(lax.broadcasted_iota(jnp.int32, score.shape, 1) <= when, score, -jnp.inf)
+        top = max_s[both, 0:1]
+        new = jnp.maximum(top, jnp.max(score, axis=1, keepdims=True))
+        fade = jnp.exp2(top * SHARP - new * SHARP)
+        p = jnp.exp2(score * SHARP - new * SHARP)
+        total = sum_s[both, 0:1] * fade + jnp.sum(p, axis=1, keepdims=True)
+        mixed = acc_s[both, :] * fade + mm(p.astype(BF), keys[:, 0:KVR])
+        mixed = (mixed / total).astype(BF)
+        for k in range(2):
+            val = mm(mixed[k * m : (k + 1) * m], wuv[k]).astype(BF)
+            for i, s in enumerate(slots):
+                there = pl.ds(pl.multiple_of(s * ROWS, ROWS), ROWS)
+                out_ref[there, 128 * k : 128 * (k + 1)] = val[ROWS * i : ROWS * (i + 1)]
+
+    finish_gather = all_gather("o", net, at, lat_part)
+    next(finish_gather)
     for _ in prefix:
         pass
     for h in range(5):
         sib_rows("p", net, at, pre_part, h)
-    for h in all_gather("o", net, at, lat_part):
-        sib_rows("o", net, at, lat_part, h)
+    for h in finish_gather:
+        if h is not None:
+            queries(h)
+    for h in range(5):
+        new_keys(h)
     net.drain()
+
+
+SHARP = float((NOPE + ROPE) ** (-0.5) * np.log2(np.e))
 
 
 def trig_table():
@@ -428,69 +531,19 @@
     return both.astype(np.float32)
 
 
-def attend_kernel(lat_ref, pre_ref, trig_ref, wuq_ref, wuk_ref, wuv_ref, out_ref, kv, qs, acc_ref, m_ref, l_ref):
-    scale = (NOPE + ROPE) ** (-0.5)
-    trig = trig_ref[...]
-    cos, sin = trig[:, 0:32], trig[:, 32:64]
-    kv[:, 0:KEY] = lat_ref[:, QR:LAT]
-    q = mm(lat_ref[:, 0:QR], wuq_ref[...])
-    for h in range(2):
-        base = h * (NOPE + ROPE)
-        nope = q[:, base : base + NOPE].astype(BF)
-        qs[h, :, 0:KVR] = mm(nope, wuk_ref[h]).astype(BF)
-        first = q[:, base + NOPE : base + NOPE + 32]
-        second = q[:, base + NOPE + 32 : base + NOPE + 64]
-        turned = jnp.concatenate([first * cos - second * sin, first * sin + second * cos], axis=1)
-        qs[h, :, KVR:KEY] = turned.astype(BF)
-    for h in range(2):
-        for i in range(2):
-            rows = pl.ds(256 * i, 256)
-            query = qs[h, rows, :]
-            for b in range(5):
-                if b < 4:
-                    keys = pre_ref[512 * b : 512 * (b + 1), :]
-                else:
-                    keys = kv[...]
-                s = mm(query, keys, NT) * scale
-                if b == 4:
-                    t = lax.broadcasted_iota(jnp.int32, s.shape, 0) + 256 * i
-                    j = lax.broadcasted_iota(jnp.int32, s.shape, 1)
-                    s = jnp.where(j <= t, s, -jnp.inf)
-                top = jnp.max(s, axis=1, keepdims=True)
-                if b == 0:
-                    m = top
-                    p = jnp.exp(s - m)
-                    l = jnp.sum(p, axis=1, keepdims=True)
-                    acc = mm(p.astype(BF), keys[:, 0:KVR])
-                else:
-                    new = jnp.maximum(m, top)
-                    fade = jnp.exp(m - new)
-                    p = jnp.exp(s - new)
-                    l = l * fade + jnp.sum(p, axis=1, keepdims=True)
-                    acc = acc * fade + mm(p.astype(BF), keys[:, 0:KVR])
-                    m = new
-            latent = (acc / l).astype(BF)
-            out_ref[rows, 128 * h : 128 * (h + 1)] = mm(latent, wuv_ref[h]).astype(BF)
-
-
 def per_device(
     sections, tokens, expert_ids, gate_values, w_gate, w_up, w_down, norm_gain, w_dq, w_dkv, q_gain, kv_gain, w_uq, w_uk,
     w_uv, prefix_cache,
 ):
-    e = lax.axis_index("expert")
-    gains = norm_gain[0].reshape(32, FB)
-    pair = jnp.stack([lax.dynamic_index_in_dim(gains, k, 0, False) for k in (e, e // 2 * 2 + 1 - e % 2)])
-    pair = jnp.broadcast_to(pair[:, :, None], (2, FB, 128))
-    table = trig_table()
     vm = pl.BlockSpec(memory_space=pltpu.VMEM)
     anyw = pl.BlockSpec(memory_space=pl.ANY)
     V = pltpu.VMEM
-    lat_rows, prefix = pl.pallas_call(
+    out = pl.pallas_call(
         functools.partial(relay_kernel, sections),
         name="relay",
-        out_shape=(jax.ShapeDtypeStruct((32, ROWS, LATW), BF), jax.ShapeDtypeStruct((32, PRE, KEY), BF)),
-        in_specs=[anyw, vm, vm, anyw, anyw, anyw, vm, anyw, anyw, vm, vm, vm, anyw],
-        out_specs=(vm, vm),
+        out_shape=jax.ShapeDtypeStruct((TOK, 256), BF),
+        in_specs=[anyw, vm, vm, anyw, anyw, anyw, vm, anyw, anyw, vm, vm, vm, anyw, anyw, anyw, anyw],
+        out_specs=vm,
         scratch_shapes=[
             V((32, ROWS, WIDE), BF),
             V((D, 2 * HID), BF),
@@ -514,33 +567,25 @@
             V((2, 4, 2, ROWS, LATW), BF),
             V((8, ROWS, LATW), BF),
             V((8, ROWS, LATW), BF),
+            V((32, ROWS, LATW), BF),
+            V((32, PRE, KEY), BF),
+            V((2, 384, 128), F32),
+            V((QR, 384), BF),
+            V((2, NOPE, KVR), BF),
+            V((2, KVR, 128), BF),
+            V((2 * TOK, KEY), BF),
+            V((2 * TOK, KVR), F32),
+            V((2 * TOK, 128), F32),
+            V((2 * TOK, 128), F32),
             pltpu.SemaphoreType.DMA((256,)),
             pltpu.SemaphoreType.DMA((256,)),
-            pltpu.SemaphoreType.DMA((8,)),
+            pltpu.SemaphoreType.DMA((16,)),
         ],
-        compiler_params=pltpu.CompilerParams(collective_id=0, has_side_effects=True, vmem_limit_bytes=58 << 20),
-        cost_estimate=pl.CostEstimate(flops=4 * 10**9, bytes_accessed=12 * 10**6, transcendentals=10**6),
+        compiler_params=pltpu.CompilerParams(collective_id=0, has_side_effects=True, vmem_limit_bytes=60 << 20),
+        cost_estimate=pl.CostEstimate(flops=12 * 10**9, bytes_accessed=12 * 10**6, transcendentals=4 * 10**6),
     )(
-        tokens[0], expert_ids[0], gate_values[0], w_gate[0], w_up[0], w_down[0], pair, w_dq[0], w_dkv[0], q_gain,
-        kv_gain, jnp.asarray(table.reshape(32, ROWS, ROPE)), prefix_cache[0],
-    )
-    out = pl.pallas_call(
-        attend_kernel,
-        name="attend",
-        out_shape=jax.ShapeDtypeStruct((TOK, 256), BF),
-        in_specs=[vm] * 6,
-        out_specs=vm,
-        scratch_shapes=[
-            V((TOK, KEY), BF),
-            V((2, TOK, KEY), BF),
-            V((8, 128), F32),
-            V((8, 128), F32),
-            V((8, 128), F32),
-        ],
-        compiler_params=pltpu.CompilerParams(vmem_limit_bytes=58 << 20),
-        cost_estimate=pl.CostEstimate(flops=9 * 10**9, bytes_accessed=8 * 10**6, transcendentals=3 * 10**6),
-    )(
-        lat_rows.reshape(TOK, LATW), prefix.reshape(CACHE, KEY), jnp.asarray(table), w_uq[0], w_uk[0], w_uv[0]
+        tokens[0], expert_ids[0].T, gate_values[0].T, w_gate[0], w_up[0], w_down[0], norm_gain, w_dq[0], w_dkv[0],
+        q_gain, kv_gain, jnp.asarray(trig_table().reshape(32, ROWS, ROPE)), prefix_cache[0], w_uq[0], w_uk[0], w_uv[0],
     )
     return out[None]
 

time: 168 us -> 142 us (0.85)
  Pallas kernels: 162 us -> 140 us
  local copies, waits for them, and re-layouts: 4.11 us -> 1.67 us
    pallas_call x1 -> x0, Pallas kernels: 16.2 us -> none  [per_device(): pl.pallas_call(attend_kernel, name='attend', out_shape=jax.ShapeDtypeStru...]
    pallas_call x1, Pallas kernels: 146 us -> 140 us  [per_device(): pl.pallas_call(functools.partial(relay_kernel, sections), name='relay', o...]
    squeeze x2 -> x0, local copies, waits for them, and re-layouts: 2.7 us -> none  [the longest x1 1.35 us: per_device(): expert_ids[0]]
where the time goes in v2:
time: 142 us
  Pallas kernels  140 us (99%)
  local copies, waits for them, and re-layouts  1.67 us (1%)
    pallas_call x1, Pallas kernels, per_device(): pl.pallas_call(functools.partial(relay_kernel, sections), name='relay', o...  140 us

profile of v2, /device:TPU:1, one launch (start us, length us, event | category | flops | bytes accessed | tf_op | source)
XLA Modules:
  0.0 141.5 jit_solution(4786931173645520913)
XLA Ops:
  0.0 139.9 %relay.1 = bf16[512,256]{1,0:T(8,128)(2,1)} custom-call(bf16[16,7168]{1,0:T(8,128)(2,1)} %bitcast.26, s32[2,16]{1,0:T(2,128)} %bitcast.28, f32[2,16]{1,0:T(2,128)} %bitcast.29, bf16[7168,128]{1,0:T(8,128)(2,1)} %bitcast.18, bf16[7168,128]{1,0:T(8,128)(2,1)} %bitcast.19, bf16[128,7168]{1,0:T(8,128)(2,1)} %bitcast.20, f32[1,7168]{1,0:T(1,128)} %gain_ref.1, ...), custom_call_target="tpu_custom_call" | custom-call | flops 12000000000 | bytes 12000000 | tf_op jit(solution)/shard_map/relay/pallas_call | solution.py:541
  139.9 1.7 %copy.18 = bf16[1,512,256]{2,1,0:T(8,128)(2,1)} copy(bf16[1,512,256]{2,1,0:T(8,128)(2,1)} %bitcast.17) | data formatting | bytes 524288

commit v3 on v2

v3 whole, which is shorter than its diff:
```python
import functools

import jax
import jax.numpy as jnp
import numpy as np
from jax import lax
from jax.experimental import pallas as pl
from jax.experimental.pallas import tpu as pltpu
from jax.sharding import PartitionSpec as P

MESH = pl.DeviceIdType.MESH
COPIES = 107
SENDS = 11
REUSED = {"o": "t", "l": "m"}
BF = jnp.bfloat16
F32 = jnp.float32
EPSILON = 1e-06
D = 7168
ROWS = 16
SIDE = 128
WIDE = D + SIDE
HID = 128
QR = 1536
KVR = 512
ROPE = 64
NOPE = 128
KEY = KVR + ROPE
LAT = QR + KEY
LATW = 2176
FB = 224
TOK = 512
CACHE = 2048
PRE = 64
KT = (((1,), (0,)), ((), ()))
NT = (((1,), (1,)), ((), ()))
TN = (((0,), (0,)), ((), ()))


def mm(a, b, dims=KT):
    return lax.dot_general(a, b, dims, preferred_element_type=F32)


class Net:
    def __init__(self, send_sems, recv_sems, places):
        self.send_sems, self.recv_sems, self.places = send_sems, recv_sems, places
        self.ids, self.groups = {}, {}

    def copy(self, key, src, dst, place, group="t"):
        same = (REUSED.get(key[0], key[0]),) + key[1:]
        index = self.ids.setdefault(same, len(self.ids))
        return pltpu.make_async_remote_copy(
            src_ref=src,
            dst_ref=dst,
            send_sem=self.send_sems.at[self.groups.setdefault(group, len(self.groups))],
            recv_sem=self.recv_sems.at[index],
            device_id=self.places[place],
            device_id_type=MESH,
        )

    def send(self, key, src, dst, place):
        self.copy(key, src, dst, place, key[0]).start()

    def wait(self, key, ref):
        self.copy(key, ref, ref, "sib").wait_recv()

    def sent(self, group, ref):
        self.copy(("t", "xA"), ref, ref, "sib", group).wait_send()


class Hops:
    def __init__(self, ref):
        self.ref, self.at = ref, self

    def __getitem__(self, index):
        first = index[0] * 8 + index[1] * 2
        return self.ref.at[first + index[2]] if len(index) == 3 else self.ref.at[pl.ds(first, 2)]


DIRS = (("R", -1), ("L", 1))


def all_gather(n, net, slot, part):
    def pass_on(key, s, what, place):
        net.send(key, part(s, what), part(s, what), place)

    me, mate = slot(0, 0, 0), slot(1, 0, 0)
    pass_on((n, "xA"), me, "A", "xp")
    for what in "BA":
        for way, _ in DIRS:
            pass_on((n, what, way, 1), me, what, way)
    pass_on((n, "xB", "", 0), me, "B", "xp")
    pass_on((n, "s0", "", 0), me, "F", "sib")
    yield []
    net.wait((n, "xA"), part(mate, "A"))
    for way, _ in DIRS:
        pass_on((n, "A1", way, 1), mate, "A", way)
    net.wait((n, "xB", "", 0), part(mate, "B"))
    pass_on((n, "s1", "", 0), mate, "F", "sib")

    def finish(h):
        if h < 4:
            for way, sign in DIRS:
                s = slot(1, sign * h, 0)
                net.wait((n, "xB", way, h), part(s, "B"))
                pass_on((n, "s1", way, h), s, "F", "sib")
        else:
            s = slot(1, 4, 0)
            net.wait((n, "xB", "R", 4), part(s, "B1"))
            net.wait((n, "xB", "L", 4), part(s, "B2"))
            pass_on((n, "s1", "R", 4), s, "F", "sib")

    for h in range(1, 5):
        for way, sign in DIRS:
            s = slot(0, sign * h, 0)
            half = "B1" if way == "R" else "B2"
            if h < 4:
                net.wait((n, "B", way, h), part(s, "B"))
                pass_on((n, "B", way, h + 1), s, "B" if h < 3 else half, way)
                pass_on((n, "xB", way, h), s, "B", "xp")
            else:
                net.wait((n, "B", way, 4), part(s, half))
                pass_on((n, "xB", way, 4), s, half, "xp")
        if h >= 2:
            finish(h - 1)
        for way, sign in DIRS:
            if h < 4 or way == "R":
                s = slot(0, sign * h, 0)
                net.wait((n, "A", way, h), part(s, "A"))
                if h < 3 or (h == 3 and way == "R"):
                    pass_on((n, "A", way, h + 1), s, "A", way)
                pass_on((n, "s0", way, h), s, "F", "sib")
        yield [(0, h - 1)] + ([(1, h - 2)] if h > 1 else [])
        for way, sign in DIRS:
            if h < 4 or way == "L":
                s = slot(1, sign * h, 0)
                net.wait((n, "A1", way, h), part(s, "A"))
                if h < 3 or (h == 3 and way == "L"):
                    pass_on((n, "A1", way, h + 1), s, "A", way)
    yield [(0, 4), (1, 3)]
    finish(4)
    yield [(1, 4)]


def sib_rows(n, net, slot, part, group):
    slots = []
    for dx, h in group:
        for way, sign in DIRS if 0 < h < 4 else (("" if h == 0 else "R", 1),):
            net.wait((n, f"s{dx}", way, h), part(slot(dx, sign * h, 1), "F"))
            slots += [slot(dx, sign * h, 0), slot(dx, sign * h, 1)]
    return slots


def reduce_scatter(n, net, value, cut, ms, mr, xs, xr, joined=False):
    order = [4, 3, -3, 2, -2, 1, -1, 0]

    def put(key, buf, there, what, val, place):
        cut(buf, what)[...] = val.astype(BF)
        net.send(key, cut(buf, what), cut(there, what), place)

    def got(key, buf, what):
        net.wait(key, cut(buf, what))
        return cut(buf, what)[...].astype(F32)

    last = ("B",) if joined else ("B1", "B2")
    trips = [(0, 1), (1, 2), (3, 2), (5, 2), (7, 1)] if joined else [(k, 1) for k in range(8)]

    def over_x(j):
        if j < len(trips):
            k, count = trips[j]
            for i in range(k, k + count):
                cut(xs.at[i], "B")[...] = value(1, order[i], "B").astype(BF)
            there = pl.ds(k, count)
            if count == 1:
                there = k
            net.send((n, "x", k), cut(xs.at[there], "B"), cut(xr.at[there], "B"), "xp")

    def from_x(i):
        for j, (k, count) in enumerate(trips):
            if k == i:
                net.wait((n, "x", k), cut(xr.at[pl.ds(k, count) if count > 1 else k], "B"))
                over_x(j + 3)

    def hop_a(h):
        for d in (1, 0):
            for w, way in enumerate("RL"):
                if h == 1 and w != d:
                    continue
                val = value(d, (5 - h) * (1 if way == "R" else -1), "A")
                if h > 2 or (h == 2 and w == d):
                    val = val + got((n, "A", way, h - 1, d), mr.at[w, h - 2, d], "A")
                put((n, "A", way, h, d), ms.at[w, h - 1, d], mr.at[w, h - 1, d], "A", val, way)

    def hop_b(h):
        for w, (way, half, rest) in enumerate((("R", "B1", "B2"), ("L", "B2", "B1"))):
            dz = (5 - h) * (1 if way == "R" else -1)
            k = order.index(dz if h > 1 else 4)
            if h > 1 or w == 0:
                from_x(k)
            buf, there = ms.at[w, h - 1, 0], mr.at[w, h - 1, 0]
            if h == 1:
                val = value(0, 4, half) + cut(xr.at[k], half)[...].astype(F32)
                put((n, "B", way, 1), buf, there, half, val, way)
            elif h == 2:
                val = value(0, dz, rest) + cut(xr.at[k], rest)[...].astype(F32)
                cut(buf, rest)[...] = val.astype(BF)
                val = value(0, dz, half) + cut(xr.at[k], half)[...].astype(F32)
                val = val + got((n, "B", way, 1), mr.at[w, 0, 0], half)
                cut(buf, half)[...] = val.astype(BF)
                net.send((n, "B", way, h), cut(buf, "B"), cut(there, "B"), way)
            else:
                net.wait((n, "B", way, h - 1), cut(mr.at[w, h - 2, 0], "B"))
                for what in last if h == 4 else ("B",):
                    val = value(0, dz, what) + cut(xr.at[k], what)[...].astype(F32)
                    val = val + cut(mr.at[w, h - 2, 0], what)[...].astype(F32)
                    put((n, "B2" if what == "B2" else "B", way, h), buf, there, what, val, way)

    over_x(0)
    hop_a(1)
    over_x(1)
    over_x(2)
    yield 1
    for h in range(2, 5):
        hop_a(h)
        hop_b(h - 1)
        yield h
    val = value(1, 0, "A")
    for w, way in enumerate("RL"):
        val = val + got((n, "A", way, 4, 1), mr.at[w, 3, 1], "A")
    put((n, "xA"), xs.at[7], xr.at[7], "A", val, "xp")
    hop_b(4)
    yield 5
    own = value(0, 0, "A")
    for w, way in enumerate("RL"):
        own = own + got((n, "A", way, 4, 0), mr.at[w, 3, 0], "A")
    yield "A", own + got((n, "xA"), xr.at[7], "A")
    from_x(7)
    for what in last:
        val = value(0, 0, what) + cut(xr.at[7], what)[...].astype(F32)
        for w, way in enumerate("RL"):
            val = val + got((n, "B2" if what == "B2" else "B", way, 4), mr.at[w, 3, 0], what)
        yield what, val


def last_cut(ref, a, b):
    return ref.at[..., pl.ds(a, b - a)]


TOK_CUTS = {"A": (0, 3456), "B": (3456, WIDE), "B1": (3456, 5376), "B2": (5376, WIDE), "F": (0, WIDE)}
LAT_CUTS = {"A": (0, 1024), "B": (1024, LATW), "B1": (1024, 1664), "B2": (1664, LATW), "F": (0, LATW)}
MIX_CUTS = {"A": (0, 96), "B": (96, 224), "B1": (96, 160), "B2": (160, 224), "F": (0, 224)}


def relay_kernel(
    sections,
    tok_ref, ids_ref, gates_ref, wg_ref, wu_ref, wd_ref, gain_ref, wq_ref, wk_ref, qg_ref, kg_ref, trig_ref, pre_ref,
    wuq_ref, wuk_ref, wuv_ref,
    out_ref,
    buf, wgu, wdn, wt, wdt, hid, hidt, toks_t, ms, mr, xs, xr, arr, arr_s, wqs, wks, lat,
    ms2, mr2, xs2, xr2, lat_out, pre_out, gcol, wuq, wuk, wuv, wx, kx, vx, qs, acc_s, max_s, sum_s, send_sems, recv_sems, local_sems,
):
    sec, e = lax.axis_index("section"), lax.axis_index("expert")
    xh, z, c = e // 16, (e // 2) % 8, e % 2

    turn = 1 - 2 * c

    def column(dz, dc=0):
        return (z + turn * (-dz if dc else dz) + 8) % 8

    def at(dx, dz, dc):
        return (xh + dx) % 2 * 16 + column(dz, dc) * 2 + (c + dc) % 2

    places = {
        "R": (sec, at(0, 1, 0)),
        "L": (sec, at(0, -1, 0)),
        "xp": (sec, at(1, 0, 0)),
        "sib": (sec, at(0, 0, 1)),
        "next": ((sec + 1) % sections, e),
        "next sib": ((sec + 1) % sections, at(0, 0, 1)),
        "prev": ((sec + sections - 1) % sections, e),
        "prev sib": ((sec + sections - 1) % sections, at(0, 0, 1)),
    }
    net = Net(send_sems, recv_sems, places)
    all_blocks, all_rows = ms.at[pl.ds(0, 15)], ms2.at[pl.ds(0, 15)]
    ms, mr, ms2, mr2 = (Hops(r) for r in (ms, mr, ms2, mr2))
    local = []

    def fetch(k, src, dst):
        cp = pltpu.make_async_copy(src, dst, local_sems.at[k])
        cp.start()
        local.append(cp)
        return cp

    def slot(dx, dz, dc):
        return (c + dc) % 2 * 16 + (xh + dx) % 2 * 8 + column(dz, dc)

    me = slot(0, 0, 0)
    own = fetch(0, tok_ref, buf.at[me, :, pl.ds(0, D)])
    load_g = fetch(1, wg_ref, wgu.at[:, pl.ds(0, HID)])
    load_u = fetch(2, wu_ref, wgu.at[:, pl.ds(HID, HID)])
    load_d = fetch(3, wd_ref, wdn)
    load_q = fetch(4, wq_ref, wqs.at[0])
    load_k = fetch(5, wk_ref, wks.at[0])
    load_p = fetch(6, pre_ref, pre_out.at[c, xh * 8 + z])
    load_uq = fetch(8, wuq_ref, wuq)
    load_uk = fetch(9, wuk_ref, wuk)
    load_uv = fetch(10, wuv_ref, wuv)

    barrier = pltpu.get_barrier_semaphore()
    for there in places.values():
        pl.semaphore_signal(barrier, inc=1, device_id=there, device_id_type=MESH)

    lane = lax.broadcasted_iota(jnp.int32, (ROWS, SIDE), 1)
    diag = lax.broadcasted_iota(jnp.int32, (ROWS, ROWS), 0) == lax.broadcasted_iota(jnp.int32, (ROWS, ROWS), 1)
    g = jnp.zeros((ROWS, SIDE), F32)
    for k in range(2):
        chosen = jnp.sum(jnp.where(diag, ids_ref[k : k + 1, :], 0), axis=1, keepdims=True)
        weight = jnp.sum(jnp.where(diag, gates_ref[k : k + 1, :], 0.0), axis=1, keepdims=True)
        g = g + jnp.where(chosen == lane % 4, weight, 0.0)
    high = g.astype(BF)
    low = (g - high.astype(F32)).astype(BF)
    side = jnp.where(lane < 4, high.astype(F32), jnp.where(lane < 8, low.astype(F32), 0.0)).astype(BF)
    buf[me, :, D:WIDE] = side

    pl.semaphore_wait(barrier, len(places))
    own.wait()

    def tok_part(s, what):
        return last_cut(buf.at[s], *TOK_CUTS[what])

    expert = e // 8
    gather = all_gather("t", net, slot, tok_part)
    next(gather)
    load_q.wait()
    net.send(("wq",), wqs.at[0], wqs.at[1], "sib")
    load_k.wait()
    net.send(("wk",), wks.at[0], wks.at[1], "sib")

    def window(owner):
        return jnp.minimum(FB * owner // 128 * 128, D - 384)

    for i in range(2):
        first = window(at(0, 0, i))
        piece = gain_ref[0:1, pl.ds(pl.multiple_of(first, 128), 384)]
        gcol[i] = jnp.broadcast_to(piece, (128, 384)).T
    load_d.wait()
    for k in range(8):
        wt[4 * k : 4 * k + 4] = wdn[:, 896 * k : 896 * (k + 1)].T.reshape(4, FB, HID)

    half = pl.ds(pl.multiple_of(c * HID, HID), HID)
    pairs = wt.reshape(16, 2, FB, HID)
    net.send(("wd",), pairs.at[:, (c + 1) % 2], wdt.at[:, :, half], "sib")
    keep_d = fetch(7, pairs.at[:, c], wdt.at[:, :, half])

    load_g.wait()
    load_u.wait()

    def experts(group):
        slots = sib_rows("t", net, slot, tok_part, group)
        m = len(slots) * ROWS
        acc = jnp.zeros((m, 2 * HID), F32)
        for k in range(7):
            rows = jnp.concatenate([buf[s, :, 1024 * k : 1024 * (k + 1)] for s in slots], axis=0)
            acc = acc + mm(rows, wgu[1024 * k : 1024 * (k + 1), :])
        side = jnp.concatenate([buf[s, :, D:WIDE] for s in slots], axis=0).astype(F32)
        lane = lax.broadcasted_iota(jnp.int32, (m, SIDE), 1)
        gate = jnp.sum(jnp.where((lane % 4 == expert) & (lane < 8), side, 0.0), axis=1, keepdims=True)
        gp, up = acc[:, :HID], acc[:, HID:]
        val = (gp / (1.0 + jnp.exp(-gp)) * up * gate).astype(BF)
        for i, s in enumerate(slots):
            hid[pl.ds(pl.multiple_of(s * ROWS, ROWS), ROWS), half] = val[ROWS * i : ROWS * (i + 1)]

    def gather_prefix():
        def chunk(dx, dz):
            return pre_out.at[c, (xh + dx) % 2 * 8 + column(dz)]

        def pass_on(key, ref, place):
            net.send(key, ref, ref, place)

        def hop(d, h):
            for way, sign in DIRS:
                if h < 4 or (way == "R") == (d == 0):
                    if h > 0:
                        net.wait(("p", d, way, h), chunk(d, sign * h))
                    if h < 3 or (h == 3 and (way == "R") == (d == 0)):
                        pass_on(("p", d, way, h + 1), chunk(d, sign * h), way)

        hop(0, 0)
        pass_on(("p", "x"), chunk(0, 0), "xp")
        yield
        hop(0, 1)
        yield
        net.wait(("p", "x"), chunk(1, 0))
        hop(1, 0)
        yield
        for d, h in ((0, 2), (0, 3), (1, 1), (0, 4), (1, 2), (1, 3), (1, 4)):
            hop(d, h)
            yield
        pass_on(("all", "sib"), pre_out.at[c], "sib")
        yield
        net.wait(("all", "sib"), pre_out.at[(c + 1) % 2])

    prefix = gather_prefix()

    def ticks(count):
        for _ in range(count):
            next(prefix, None)

    for group in gather:
        if group == [(0, 3), (1, 2)]:
            load_p.wait()
            ticks(1)
        if group == [(1, 4)]:
            ticks(1)
        experts(group)
    net.send(("hid",), hid.at[:, half], hid.at[:, half], "sib")
    ticks(1)

    start = window(e)
    toks_t[...] = buf[:, :, pl.ds(pl.multiple_of(start, 128), 384)].reshape(TOK, 384).T

    load_uk.wait()
    load_uv.wait()
    for k in range(2):
        wx[:, 128 * k : 128 * (k + 1)] = wuv[k]

    other = pl.ds(pl.multiple_of((c + 1) % 2 * HID, HID), HID)
    net.wait(("hid",), hid.at[:, other])
    net.wait(("wd",), wdt.at[:, :, other])
    keep_d.wait()
    hidt[...] = hid[...].T

    def mixed_term(dx, dz, what):
        a, b = MIX_CUTS[what]
        block = (xh + dx) % 2 * 8 + column(dz)
        return mm(wdt[block, a:b, :], hidt[...])

    def mix_cut(ref, what):
        a, b = MIX_CUTS[what]
        return ref.at[pl.ds(a, b - a)]

    off = FB * e - start
    for got in reduce_scatter("m", net, mixed_term, mix_cut, ms, mr, xs, xr):
        if not isinstance(got, tuple):
            ticks({1: 1, 5: 2}.get(got, 0))
            continue
        what, val = got
        a, b = MIX_CUTS[what]
        rows = toks_t[pl.ds(pl.multiple_of(off + a, 16), b - a), :].astype(F32)
        arr_s[a:b] = (val + rows).astype(BF)
        for i, place in enumerate(("next", "next sib")):
            tokens_of = pl.ds(pl.multiple_of((c + i) % 2 * 256, 256), 256)
            block = arr_s.at[pl.ds(a, b - a), tokens_of]
            net.send(("next", i, what), block, arr.at[i, pl.ds(a, b - a)], place)

    ticks(2)
    net.wait(("wq",), wqs.at[1])
    net.wait(("wk",), wks.at[1])
    squares = jnp.zeros((1, 256), F32)
    for i in range(2):
        for what in ("A", "B1", "B2"):
            net.wait(("next", i, what), mix_cut(arr.at[i], what))
        x = arr[i].astype(F32)
        squares = squares + jnp.sum(x * x, axis=0, keepdims=True)
        shift = FB * at(0, 0, i) - window(at(0, 0, i))
        scaled = (x * gcol[i, pl.ds(pl.multiple_of(shift, 32), FB), 0:1]).T.astype(BF)
        if i == 0:
            lat[:, 0:QR] = mm(scaled, wqs[0])
            lat[:, QR:LAT] = mm(scaled, wks[0])
        else:
            lat[:, 0:QR] += mm(scaled, wqs[1])
            lat[:, QR:LAT] += mm(scaled, wks[1])
    lat[:, LAT:LATW] = jnp.broadcast_to(squares, (128, 256)).T[:, 0 : LATW - LAT]

    def lat_term(dx, dz, what):
        a, b = LAT_CUTS[what]
        block = (xh + dx) % 2 * 8 + column(dz)
        return lat[pl.ds(pl.multiple_of(block * ROWS, ROWS), ROWS), a:b]

    def lat_cut(ref, what):
        return last_cut(ref, *LAT_CUTS[what])

    ticks(1)
    sums = {}
    for got in reduce_scatter("l", net, lat_term, lat_cut, ms2, mr2, xs2, xr2, True):
        if isinstance(got, tuple):
            sums[got[0]] = got[1]
        elif got == 3:
            ticks(2)
    total = jnp.concatenate([sums["A"], sums["B"]], axis=1)
    scale = lax.rsqrt(total[:, LAT : LAT + 1] * (1.0 / D) + EPSILON)

    def rms(v, gain):
        v = v * scale
        return (v * lax.rsqrt(jnp.mean(v * v, axis=1, keepdims=True) + EPSILON) * gain).astype(BF)

    lat_out[e, :, 0:QR] = rms(total[:, 0:QR], qg_ref[...])
    lat_out[e, :, QR : QR + KVR] = rms(total[:, QR : QR + KVR], kg_ref[...])
    tail = total[:, QR + KVR :] * scale
    first, second = tail[:, 0:32], tail[:, 32:64]
    cos, sin = trig_ref[e, :, 0:32], trig_ref[e, :, 32:64]
    turned = jnp.concatenate([first * cos - second * sin, first * sin + second * cos], axis=1)
    lat_out[e, :, QR + KVR : LAT] = turned.astype(BF)
    lat_out[e, :, LAT:LATW] = jnp.zeros((ROWS, LATW - LAT), BF)

    def lat_part(s, what):
        return last_cut(lat_out.at[s], *LAT_CUTS[what])

    load_uq.wait()
    order = []

    def expand(first, rows):
        there = slice(first, first + 512)
        values = mm(rows[:, 0:KVR], wx[...]).astype(BF)
        for k in range(2):
            kx[k, 0:NOPE, there] = mm(wuk[k], rows[:, 0:KVR], NT).astype(BF)
            kx[k, NOPE:, there] = rows[:, KVR:KEY].T
            vx[k, there, :] = values[:, 128 * k : 128 * (k + 1)]

    def queries(group):
        slots = sib_rows("o", net, at, lat_part, group)
        m = len(slots) * ROWS
        base = len(order) * ROWS
        order.extend(slots)
        mine = slice(base, base + m)
        angle = jnp.concatenate([trig_ref[s] for s in slots], axis=0)
        cos, sin = angle[:, 0:32], angle[:, 32:64]
        q = mm(jnp.concatenate([lat_out[s, :, 0:QR] for s in slots], axis=0), wuq[...]) * SHARP
        for k in range(2):
            a = k * (NOPE + ROPE)
            first, second = q[:, a + NOPE : a + NOPE + 32], q[:, a + NOPE + 32 : a + NOPE + 64]
            turned = jnp.concatenate([first * cos - second * sin, first * sin + second * cos], axis=1)
            qs[k, mine, 0:NOPE] = q[:, a : a + NOPE].astype(BF)
            qs[k, mine, NOPE:] = turned.astype(BF)
        both = range(2)
        score = [[mm(qs[k, mine, :], kx[k, :, 512 * b : 512 * (b + 1)]) for b in range(4)] for k in both]
        top = [functools.reduce(jnp.maximum, [jnp.max(x, axis=1, keepdims=True) for x in score[k]]) for k in both]
        for k in both:
            total, mixed = 0.0, 0.0
            for b in range(4):
                p = jnp.exp2(score[k][b] - top[k])
                total = total + jnp.sum(p, axis=1, keepdims=True)
                mixed = mixed + mm(p.astype(BF), vx[k, 512 * b : 512 * (b + 1), :])
            acc_s[k, mine, :] = mixed
            max_s[k, mine, :] = jnp.broadcast_to(top[k], (m, 128))
            sum_s[k, mine, :] = jnp.broadcast_to(total, (m, 128))

    def new_keys():
        row = lax.broadcasted_iota(jnp.int32, (ROWS, 1), 0)
        when = jnp.concatenate([row + s * ROWS for s in order], axis=0)
        key_when = lax.broadcasted_iota(jnp.int32, (1, TOK), 1)
        pieces = [(k, slice(256 * i, 256 * (i + 1))) for i in range(2) for k in range(2)]
        score = [mm(qs[k, mine, :], kx[k, :, CACHE:]) for k, mine in pieces]
        score = [jnp.where(key_when <= when[mine], x, -jnp.inf) for x, (k, mine) in zip(score, pieces)]
        new = [jnp.maximum(max_s[k, mine, 0:1], jnp.max(x, axis=1, keepdims=True)) for x, (k, mine) in zip(score, pieces)]
        for (k, mine), x, top in zip(pieces, score, new):
            fade = jnp.exp2(max_s[k, mine, 0:1] - top)
            p = jnp.exp2(x - top)
            total = sum_s[k, mine, 0:1] * fade + jnp.sum(p, axis=1, keepdims=True)
            mixed = acc_s[k, mine, :] * fade + mm(p.astype(BF), vx[k, CACHE:, :])
            val = (mixed * (1.0 / total)).astype(BF)
            for j, s in enumerate(order[mine.start // ROWS : mine.stop // ROWS]):
                there = pl.ds(pl.multiple_of(s * ROWS, ROWS), ROWS)
                out_ref[there, 128 * k : 128 * (k + 1)] = val[ROWS * j : ROWS * (j + 1)]

    finish_gather = all_gather("o", net, at, lat_part)
    next(finish_gather)
    ticks(1)
    for b in range(4):
        expand(512 * b, pre_out[b // 2, b % 2 * 8 : b % 2 * 8 + 8].reshape(512, KEY))
    for group in finish_gather:
        queries(group)
    expand(CACHE, lat_out[:, :, QR:LAT].reshape(TOK, KEY))
    new_keys()
    for group, ref in (
        ("t", buf.at[pl.ds(0, 31)]),
        ("o", lat_out.at[pl.ds(0, 31)]),
        ("m", all_blocks),
        ("l", all_rows),
        ("p", pre_out.at[0, pl.ds(0, 15)]),
        ("all", pre_out.at[0]),
        ("next", arr_s),
        ("wq", wqs.at[0]),
        ("wk", wks.at[0]),
        ("wd", wdt.at[:, :, half]),
        ("hid", hid.at[:, half]),
    ):
        net.sent(group, ref)
    assert (len(net.ids), len(net.groups)) == (COPIES, SENDS)


SHARP = float((NOPE + ROPE) ** (-0.5) * np.log2(np.e))


def trig_table():
    half = ROPE // 2
    frequency = 10000.0 ** (-np.arange(half) / half)
    angles = (CACHE + np.arange(TOK))[:, None] * frequency[None, :].astype(np.float32)
    angles = angles.astype(np.float32).astype(np.float64)
    both = np.concatenate([np.cos(angles), np.sin(angles)], axis=1)
    return both.astype(np.float32)


def per_device(
    sections, tokens, expert_ids, gate_values, w_gate, w_up, w_down, norm_gain, w_dq, w_dkv, q_gain, kv_gain, w_uq, w_uk,
    w_uv, prefix_cache,
):
    vm = pl.BlockSpec(memory_space=pltpu.VMEM)
    anyw = pl.BlockSpec(memory_space=pl.ANY)
    V = pltpu.VMEM
    out = pl.pallas_call(
        functools.partial(relay_kernel, sections),
        name="relay",
        out_shape=jax.ShapeDtypeStruct((TOK, 256), BF),
        in_specs=[anyw, vm, vm, anyw, anyw, anyw, vm, anyw, anyw, vm, vm, vm, anyw, anyw, anyw, anyw],
        out_specs=vm,
        scratch_shapes=[
            V((32, ROWS, WIDE), BF),
            V((D, 2 * HID), BF),
            V((HID, D), BF),
            V((32, FB, HID), BF),
            V((16, FB, 2 * HID), BF),
            V((TOK, 2 * HID), BF),
            V((2 * HID, TOK), BF),
            V((384, TOK), BF),
            V((16, FB, TOK), BF),
            V((16, FB, TOK), BF),
            V((8, FB, TOK), BF),
            V((8, FB, TOK), BF),
            V((2, FB, TOK // 2), BF),
            V((FB, TOK), BF),
            V((2, FB, QR), BF),
            V((2, FB, KEY), BF),
            V((TOK // 2, LATW), F32),
            V((16, ROWS, LATW), BF),
            V((16, ROWS, LATW), BF),
            V((8, ROWS, LATW), BF),
            V((8, ROWS, LATW), BF),
            V((32, ROWS, LATW), BF),
            V((2, 16, PRE, KEY), BF),
            V((2, 384, 128), F32),
            V((QR, 384), BF),
            V((2, NOPE, KVR), BF),
            V((2, KVR, 128), BF),
            V((KVR, 256), BF),
            V((2, NOPE + ROPE, CACHE + TOK), BF),
            V((2, CACHE + TOK, 128), BF),
            V((2, TOK, NOPE + ROPE), BF),
            V((2, TOK, 128), F32),
            V((2, TOK, 128), F32),
            V((2, TOK, 128), F32),
            pltpu.SemaphoreType.DMA((SENDS,)),
            pltpu.SemaphoreType.DMA((COPIES,)),
            pltpu.SemaphoreType.DMA((11,)),
        ],
        compiler_params=pltpu.CompilerParams(collective_id=0, has_side_effects=True, vmem_limit_bytes=60 << 20),
        cost_estimate=pl.CostEstimate(flops=12 * 10**9, bytes_accessed=12 * 10**6, transcendentals=4 * 10**6),
    )(
        tokens[0], expert_ids[0].T, gate_values[0].T, w_gate[0], w_up[0], w_down[0], norm_gain, w_dq[0], w_dkv[0],
        q_gain, kv_gain, jnp.asarray(trig_table().reshape(32, ROWS, ROPE)), prefix_cache[0], w_uq[0], w_uk[0], w_uv[0],
    )
    return out[None]


def solution(mesh):
    placed = (
        P("section", "expert", None),
        P("section", "expert", None),
        P("section", "expert", None),
        P("section", None, "expert"),
        P("section", None, "expert"),
        P("section", "expert", None),
        P("section", None),
        P("section", "expert", None),
        P("section", "expert", None),
        P("section", None),
        P("section", None),
        P("section", None, "expert"),
        P("section", "expert", None, None),
        P("section", "expert", None, None),
        P("section", "expert", None),
    )
    return jax.shard_map(
        functools.partial(per_device, mesh.shape["section"]),
        mesh=mesh,
        in_specs=placed,
        out_specs=P("section", None, "expert"),
        check_vma=False,
    )
```

time: 142 us -> 130 us (0.915)
  Pallas kernels: 140 us -> 128 us
    pallas_call x1, Pallas kernels: 140 us -> 128 us  [per_device(): pl.pallas_call(functools.partial(relay_kernel, sections), name='relay', o...]
where the time goes in v3:
time: 130 us
  Pallas kernels  128 us (98%)
  local copies, waits for them, and re-layouts  1.67 us (1%)
    pallas_call x1, Pallas kernels, per_device(): pl.pallas_call(functools.partial(relay_kernel, sections), name='relay', o...  128 us

profile of v3, /device:TPU:1, one launch (start us, length us, event | category | flops | bytes accessed | tf_op | source)
XLA Modules:
  0.0 130.1 jit_solution(18350264295751505248)
XLA Ops:
  0.0 128.5 %relay.1 = bf16[512,256]{1,0:T(8,128)(2,1)} custom-call(bf16[16,7168]{1,0:T(8,128)(2,1)} %bitcast.26, s32[2,16]{1,0:T(2,128)} %bitcast.28, f32[2,16]{1,0:T(2,128)} %bitcast.29, bf16[7168,128]{1,0:T(8,128)(2,1)} %bitcast.18, bf16[7168,128]{1,0:T(8,128)(2,1)} %bitcast.19, bf16[128,7168]{1,0:T(8,128)(2,1)} %bitcast.20, f32[1,7168]{1,0:T(1,128)} %gain_ref.1, ...), custom_call_target="tpu_custom_call" | custom-call | flops 12000000000 | bytes 12000000 | tf_op jit(solution)/shard_map/relay/pallas_call | solution.py:610
  128.5 1.7 %copy.18 = bf16[1,512,256]{2,1,0:T(8,128)(2,1)} copy(bf16[1,512,256]{2,1,0:T(8,128)(2,1)} %bitcast.17) | data formatting | bytes 524288

commit v4 on v3

--- a/solution.py
+++ b/solution.py
@@ -91,6 +91,7 @@
     pass_on((n, "xB", "", 0), me, "B", "xp")
     pass_on((n, "s0", "", 0), me, "F", "sib")
     yield []
+
     net.wait((n, "xA"), part(mate, "A"))
     for way, _ in DIRS:
         pass_on((n, "A1", way, 1), mate, "A", way)
@@ -109,6 +110,14 @@
             net.wait((n, "xB", "L", 4), part(s, "B2"))
             pass_on((n, "s1", "R", 4), s, "F", "sib")
 
+    def second(h):
+        for way, sign in DIRS:
+            if h < 4 or way == "L":
+                s = slot(1, sign * h, 0)
+                net.wait((n, "A1", way, h), part(s, "A"))
+                if h < 3 or (h == 3 and way == "L"):
+                    pass_on((n, "A1", way, h + 1), s, "A", way)
+
     for h in range(1, 5):
         for way, sign in DIRS:
             s = slot(0, sign * h, 0)
@@ -120,7 +129,7 @@
             else:
                 net.wait((n, "B", way, 4), part(s, half))
                 pass_on((n, "xB", way, 4), s, half, "xp")
-        if h >= 2:
+        if h > 1:
             finish(h - 1)
         for way, sign in DIRS:
             if h < 4 or way == "R":
@@ -130,15 +139,93 @@
                     pass_on((n, "A", way, h + 1), s, "A", way)
                 pass_on((n, "s0", way, h), s, "F", "sib")
         yield [(0, h - 1)] + ([(1, h - 2)] if h > 1 else [])
-        for way, sign in DIRS:
-            if h < 4 or way == "L":
-                s = slot(1, sign * h, 0)
-                net.wait((n, "A1", way, h), part(s, "A"))
-                if h < 3 or (h == 3 and way == "L"):
-                    pass_on((n, "A1", way, h + 1), s, "A", way)
+        if h < 4:
+            second(h)
+    second(4)
     yield [(0, 4), (1, 3)]
     finish(4)
     yield [(1, 4)]
+
+
+def gather_far(n, net, slot, part):
+    def pass_on(key, s, what, place):
+        net.send(key, part(s, what), part(s, what), place)
+
+    def both_ways(name, h, s, what):
+        for way, _ in DIRS:
+            pass_on((n, name, way, h), s, what, way + "2" if h == 2 else way)
+
+    me, mate = slot(0, 0, 0), slot(1, 0, 0)
+    pass_on((n, "xA"), me, "A", "xp")
+    for what in "BA":
+        both_ways(what, 2, me, what)
+        both_ways(what, 1, me, what)
+    pass_on((n, "xB", "", 0), me, "B", "xp")
+    pass_on((n, "s0", "", 0), me, "F", "sib")
+    yield []
+    net.wait((n, "xA"), part(mate, "A"))
+    both_ways("A1", 2, mate, "A")
+    both_ways("A1", 1, mate, "A")
+    net.wait((n, "xB", "", 0), part(mate, "B"))
+    pass_on((n, "s1", "", 0), mate, "F", "sib")
+
+    def ring_b(h):
+        for way, sign in DIRS:
+            s = slot(0, sign * h, 0)
+            half = "B1" if way == "R" else "B2"
+            what = "B" if h < 4 else half
+            net.wait((n, "B", way, h), part(s, what))
+            if h == 2:
+                pass_on((n, "B", way, 3), s, "B", way)
+                pass_on((n, "B", way, 4), s, half, way + "2")
+            pass_on((n, "xB", way, h), s, what, "xp")
+
+    def ring_a(name, h, d):
+        for way, sign in DIRS:
+            last = (way == "R") == (d == 0)
+            if h < 4 or last:
+                s = slot(d, sign * h, 0)
+                net.wait((n, name, way, h), part(s, "A"))
+                if h == 2:
+                    pass_on((n, name, way, 3), s, "A", way)
+                    if last:
+                        pass_on((n, name, way, 4), s, "A", way + "2")
+                if d == 0:
+                    pass_on((n, "s0", way, h), s, "F", "sib")
+
+    def finish(h):
+        if h < 4:
+            for way, sign in DIRS:
+                s = slot(1, sign * h, 0)
+                net.wait((n, "xB", way, h), part(s, "B"))
+                pass_on((n, "s1", way, h), s, "F", "sib")
+        else:
+            s = slot(1, 4, 0)
+            net.wait((n, "xB", "R", 4), part(s, "B1"))
+            net.wait((n, "xB", "L", 4), part(s, "B2"))
+            pass_on((n, "s1", "R", 4), s, "F", "sib")
+
+    ring_b(1)
+    ring_b(2)
+    ring_a("A", 1, 0)
+    ring_a("A", 2, 0)
+    yield [(0, 0)]
+    ring_a("A1", 1, 1)
+    ring_a("A1", 2, 1)
+    finish(1)
+    finish(2)
+    yield [(1, 0), (0, 1), (0, 2)]
+    ring_b(3)
+    ring_b(4)
+    ring_a("A", 3, 0)
+    ring_a("A", 4, 0)
+    yield [(1, 1), (1, 2)]
+    ring_a("A1", 3, 1)
+    ring_a("A1", 4, 1)
+    finish(3)
+    yield [(0, 3), (0, 4)]
+    finish(4)
+    yield [(1, 3), (1, 4)]
 
 
 def sib_rows(n, net, slot, part, group):
@@ -150,7 +237,7 @@
     return slots
 
 
-def reduce_scatter(n, net, value, cut, ms, mr, xs, xr, joined=False):
+def reduce_scatter(n, net, value, cut, ms, mr, xs, xr):
     order = [4, 3, -3, 2, -2, 1, -1, 0]
 
     def put(key, buf, there, what, val, place):
@@ -161,8 +248,8 @@
         net.wait(key, cut(buf, what))
         return cut(buf, what)[...].astype(F32)
 
-    last = ("B",) if joined else ("B1", "B2")
-    trips = [(0, 1), (1, 2), (3, 2), (5, 2), (7, 1)] if joined else [(k, 1) for k in range(8)]
+    last = ("B1", "B2")
+    trips = [(k, 1) for k in range(8)]
 
     def over_x(j):
         if j < len(trips):
@@ -241,6 +328,105 @@
         yield what, val
 
 
+def scatter_far(n, net, value, cut, ms, mr, xs, xr):
+    order = [4, 3, -3, 2, -2, 1, -1, 0]
+    trips = [(0, 1), (1, 2), (3, 2), (5, 2), (7, 1)]
+
+    def put(key, buf, there, what, val, place):
+        cut(buf, what)[...] = val.astype(BF)
+        net.send(key, cut(buf, what), cut(there, what), place)
+
+    def got(key, buf, what):
+        net.wait(key, cut(buf, what))
+        return cut(buf, what)[...].astype(F32)
+
+    def over_x(j):
+        if j < len(trips):
+            k, count = trips[j]
+            for i in range(k, k + count):
+                cut(xs.at[i], "B")[...] = value(1, order[i], "B").astype(BF)
+            there = pl.ds(k, count) if count > 1 else k
+            net.send((n, "x", k), cut(xs.at[there], "B"), cut(xr.at[there], "B"), "xp")
+
+    def from_x(j):
+        k, count = trips[j]
+        net.wait((n, "x", k), cut(xr.at[pl.ds(k, count) if count > 1 else k], "B"))
+        over_x(j + 3)
+
+    def place(way, h):
+        return way + "2" if h in (1, 3) else way
+
+    def send_a(h):
+        for d in (1, 0):
+            for w, way in enumerate("RL"):
+                if h == 1 and w != d:
+                    continue
+                val = value(d, (5 - h) * (1 if way == "R" else -1), "A")
+                if h == 3:
+                    val = val + got((n, "A", way, 2, d), mr.at[w, 1, d], "A")
+                    if w == d:
+                        val = val + got((n, "A", way, 1, d), mr.at[w, 0, d], "A")
+                put((n, "A", way, h, d), ms.at[w, h - 1, d], mr.at[w, h - 1, d], "A", val, place(way, h))
+
+    def send_b(h):
+        for w, (way, half, rest) in enumerate((("R", "B1", "B2"), ("L", "B2", "B1"))):
+            dz = (5 - h) * (1 if way == "R" else -1)
+            k = order.index(dz if h > 1 else 4)
+            buf, there = ms.at[w, h - 1, 0], mr.at[w, h - 1, 0]
+
+            def mine(what):
+                return value(0, dz, what) + cut(xr.at[k], what)[...].astype(F32)
+
+            if h == 3:
+                net.wait((n, "B", way, 2), cut(mr.at[w, 1, 0], "B"))
+                val = mine(rest) + cut(mr.at[w, 1, 0], rest)[...].astype(F32)
+                cut(buf, rest)[...] = val.astype(BF)
+                val = mine(half) + cut(mr.at[w, 1, 0], half)[...].astype(F32)
+                val = val + got((n, "B", way, 1), mr.at[w, 0, 0], half)
+                cut(buf, half)[...] = val.astype(BF)
+                net.send((n, "B", way, h), cut(buf, "B"), cut(there, "B"), place(way, h))
+            else:
+                what = half if h == 1 else "B"
+                put((n, "B", way, h), buf, there, what, mine(what), place(way, h))
+
+    over_x(0)
+    send_a(1)
+    send_a(2)
+    over_x(1)
+    over_x(2)
+    yield 1
+    from_x(0)
+    send_b(1)
+    from_x(1)
+    send_b(2)
+    send_a(4)
+    yield 2
+    send_a(3)
+    yield 3
+    from_x(2)
+    send_b(3)
+    from_x(3)
+    send_b(4)
+    yield 4
+    val = value(1, 0, "A")
+    for w, way in enumerate("RL"):
+        for h in (4, 3):
+            val = val + got((n, "A", way, h, 1), mr.at[w, h - 1, 1], "A")
+    put((n, "xA"), xs.at[7], xr.at[7], "A", val, "xp")
+    yield 5
+    own = value(0, 0, "A")
+    for w, way in enumerate("RL"):
+        for h in (4, 3):
+            own = own + got((n, "A", way, h, 0), mr.at[w, h - 1, 0], "A")
+    from_x(4)
+    val = value(0, 0, "B") + cut(xr.at[7], "B")[...].astype(F32)
+    for w, way in enumerate("RL"):
+        for h in (4, 3):
+            val = val + got((n, "B", way, h), mr.at[w, h - 1, 0], "B")
+    yield "B", val
+    yield "A", own + got((n, "xA"), xr.at[7], "A")
+
+
 def last_cut(ref, a, b):
     return ref.at[..., pl.ds(a, b - a)]
 
@@ -272,6 +458,8 @@
     places = {
         "R": (sec, at(0, 1, 0)),
         "L": (sec, at(0, -1, 0)),
+        "R2": (sec, at(0, 2, 0)),
+        "L2": (sec, at(0, -2, 0)),
         "xp": (sec, at(1, 0, 0)),
         "sib": (sec, at(0, 0, 1)),
         "next": ((sec + 1) % sections, e),
@@ -412,8 +600,9 @@
         if group == [(1, 4)]:
             ticks(1)
         experts(group)
+        if group == [(0, 4), (1, 3)]:
+            ticks(1)
     net.send(("hid",), hid.at[:, half], hid.at[:, half], "sib")
-    ticks(1)
 
     start = window(e)
     toks_t[...] = buf[:, :, pl.ds(pl.multiple_of(start, 128), 384)].reshape(TOK, 384).T
@@ -479,13 +668,35 @@
     def lat_cut(ref, what):
         return last_cut(ref, *LAT_CUTS[what])
 
-    ticks(1)
+    load_uq.wait()
+    order = []
+
+    def expand(first, rows):
+        there = slice(first, first + 512)
+        values = mm(rows[:, 0:KVR], wx[...]).astype(BF)
+        for k in range(2):
+            kx[k, 0:NOPE, there] = mm(wuk[k], rows[:, 0:KVR], NT).astype(BF)
+            kx[k, NOPE:, there] = rows[:, KVR:KEY].T
+            vx[k, there, :] = values[:, 128 * k : 128 * (k + 1)]
+
+    def expand_prefix(i):
+        expand(512 * i, pre_out[(c + i // 2) % 2, i % 2 * 8 : i % 2 * 8 + 8].reshape(512, KEY))
+
     sums = {}
-    for got in reduce_scatter("l", net, lat_term, lat_cut, ms2, mr2, xs2, xr2, True):
+    for got in scatter_far("l", net, lat_term, lat_cut, ms2, mr2, xs2, xr2):
         if isinstance(got, tuple):
             sums[got[0]] = got[1]
+        elif got == 1:
+            ticks(1)
         elif got == 3:
             ticks(2)
+            expand_prefix(0)
+        elif got == 4:
+            expand_prefix(1)
+        elif got == 5:
+            ticks(1)
+            expand_prefix(2)
+            expand_prefix(3)
     total = jnp.concatenate([sums["A"], sums["B"]], axis=1)
     scale = lax.rsqrt(total[:, LAT : LAT + 1] * (1.0 / D) + EPSILON)
 
@@ -504,17 +715,6 @@
 
     def lat_part(s, what):
         return last_cut(lat_out.at[s], *LAT_CUTS[what])
-
-    load_uq.wait()
-    order = []
-
-    def expand(first, rows):
-        there = slice(first, first + 512)
-        values = mm(rows[:, 0:KVR], wx[...]).astype(BF)
-        for k in range(2):
-            kx[k, 0:NOPE, there] = mm(wuk[k], rows[:, 0:KVR], NT).astype(BF)
-            kx[k, NOPE:, there] = rows[:, KVR:KEY].T
-            vx[k, there, :] = values[:, 128 * k : 128 * (k + 1)]
 
     def queries(group):
         slots = sib_rows("o", net, at, lat_part, group)
@@ -562,11 +762,8 @@
                 there = pl.ds(pl.multiple_of(s * ROWS, ROWS), ROWS)
                 out_ref[there, 128 * k : 128 * (k + 1)] = val[ROWS * j : ROWS * (j + 1)]
 
-    finish_gather = all_gather("o", net, at, lat_part)
+    finish_gather = gather_far("o", net, at, lat_part)
     next(finish_gather)
-    ticks(1)
-    for b in range(4):
-        expand(512 * b, pre_out[b // 2, b % 2 * 8 : b % 2 * 8 + 8].reshape(512, KEY))
     for group in finish_gather:
         queries(group)
     expand(CACHE, lat_out[:, :, QR:LAT].reshape(TOK, KEY))

time: 130 us -> 125 us (0.962)
  Pallas kernels: 128 us -> 124 us
    pallas_call x1, Pallas kernels: 128 us -> 124 us  [per_device(): pl.pallas_call(functools.partial(relay_kernel, sections), name='relay', o...]
where the time goes in v4:
time: 125 us
  Pallas kernels  124 us (99%)
  local copies, waits for them, and re-layouts  1.67 us (1%)
    pallas_call x1, Pallas kernels, per_device(): pl.pallas_call(functools.partial(relay_kernel, sections), name='relay', o...  124 us

profile of v4, /device:TPU:1, one launch (start us, length us, event | category | flops | bytes accessed | tf_op | source)
XLA Modules:
  0.0 125.3 jit_solution(11099715490465582648)
XLA Ops:
  0.0 123.7 %relay.1 = bf16[512,256]{1,0:T(8,128)(2,1)} custom-call(bf16[16,7168]{1,0:T(8,128)(2,1)} %bitcast.26, s32[2,16]{1,0:T(2,128)} %bitcast.28, f32[2,16]{1,0:T(2,128)} %bitcast.29, bf16[7168,128]{1,0:T(8,128)(2,1)} %bitcast.18, bf16[7168,128]{1,0:T(8,128)(2,1)} %bitcast.19, bf16[128,7168]{1,0:T(8,128)(2,1)} %bitcast.20, f32[1,7168]{1,0:T(1,128)} %gain_ref.1, ...), custom_call_target="tpu_custom_call" | custom-call | flops 12000000000 | bytes 12000000 | tf_op jit(solution)/shard_map/relay/pallas_call | solution.py:807
  123.7 1.7 %copy.18 = bf16[1,512,256]{2,1,0:T(8,128)(2,1)} copy(bf16[1,512,256]{2,1,0:T(8,128)(2,1)} %bitcast.17) | data formatting | bytes 524288

commit v5 on v4

--- a/solution.py
+++ b/solution.py
@@ -220,10 +220,10 @@
     ring_a("A", 3, 0)
     ring_a("A", 4, 0)
     yield [(1, 1), (1, 2)]
+    yield [(0, 3), (0, 4)]
     ring_a("A1", 3, 1)
     ring_a("A1", 4, 1)
     finish(3)
-    yield [(0, 3), (0, 4)]
     finish(4)
     yield [(1, 3), (1, 4)]
 
@@ -267,10 +267,10 @@
                 net.wait((n, "x", k), cut(xr.at[pl.ds(k, count) if count > 1 else k], "B"))
                 over_x(j + 3)
 
-    def hop_a(h):
+    def hop_a(h, apart=False):
         for d in (1, 0):
             for w, way in enumerate("RL"):
-                if h == 1 and w != d:
+                if (h == 1 and w != d) or (h == 2 and (w != d) != apart):
                     continue
                 val = value(d, (5 - h) * (1 if way == "R" else -1), "A")
                 if h > 2 or (h == 2 and w == d):
@@ -303,6 +303,7 @@
 
     over_x(0)
     hop_a(1)
+    hop_a(2, True)
     over_x(1)
     over_x(2)
     yield 1
@@ -580,7 +581,7 @@
         net.wait(("p", "x"), chunk(1, 0))
         hop(1, 0)
         yield
-        for d, h in ((0, 2), (0, 3), (1, 1), (0, 4), (1, 2), (1, 3), (1, 4)):
+        for d, h in ((0, 2), (1, 1), (0, 3), (1, 2), (0, 4), (1, 3), (1, 4)):
             hop(d, h)
             yield
         pass_on(("all", "sib"), pre_out.at[c], "sib")
@@ -630,7 +631,7 @@
     off = FB * e - start
     for got in reduce_scatter("m", net, mixed_term, mix_cut, ms, mr, xs, xr):
         if not isinstance(got, tuple):
-            ticks({1: 1, 5: 2}.get(got, 0))
+            ticks({5: 2}.get(got, 0))
             continue
         what, val = got
         a, b = MIX_CUTS[what]
@@ -641,11 +642,12 @@
             block = arr_s.at[pl.ds(a, b - a), tokens_of]
             net.send(("next", i, what), block, arr.at[i, pl.ds(a, b - a)], place)
 
-    ticks(2)
     net.wait(("wq",), wqs.at[1])
     net.wait(("wk",), wks.at[1])
     squares = jnp.zeros((1, 256), F32)
     for i in range(2):
+        if i == 1:
+            ticks(2)
         for what in ("A", "B1", "B2"):
             net.wait(("next", i, what), mix_cut(arr.at[i], what))
         x = arr[i].astype(F32)
@@ -687,7 +689,7 @@
         if isinstance(got, tuple):
             sums[got[0]] = got[1]
         elif got == 1:
-            ticks(1)
+            ticks(2)
         elif got == 3:
             ticks(2)
             expand_prefix(0)

time: 125 us -> 125 us (level)
  no operation moved by 1% of the time
where the time goes in v5:
time: 125 us
  Pallas kernels  124 us (99%)
  local copies, waits for them, and re-layouts  1.67 us (1%)
    pallas_call x1, Pallas kernels, per_device(): pl.pallas_call(functools.partial(relay_kernel, sections), name='relay', o...  124 us

profile of v5, /device:TPU:1, one launch (start us, length us, event | category | flops | bytes accessed | tf_op | source)
XLA Modules:
  0.0 125.4 jit_solution(16369282006927636876)
XLA Ops:
  0.0 123.7 %relay.1 = bf16[512,256]{1,0:T(8,128)(2,1)} custom-call(bf16[16,7168]{1,0:T(8,128)(2,1)} %bitcast.26, s32[2,16]{1,0:T(2,128)} %bitcast.28, f32[2,16]{1,0:T(2,128)} %bitcast.29, bf16[7168,128]{1,0:T(8,128)(2,1)} %bitcast.18, bf16[7168,128]{1,0:T(8,128)(2,1)} %bitcast.19, bf16[128,7168]{1,0:T(8,128)(2,1)} %bitcast.20, f32[1,7168]{1,0:T(1,128)} %gain_ref.1, ...), custom_call_target="tpu_custom_call" | custom-call | flops 12000000000 | bytes 12000000 | tf_op jit(solution)/shard_map/relay/pallas_call | solution.py:809
  123.7 1.7 %copy.18 = bf16[1,512,256]{2,1,0:T(8,128)(2,1)} copy(bf16[1,512,256]{2,1,0:T(8,128)(2,1)} %bitcast.17) | data formatting | bytes 524288

commit v6 on v5

--- a/solution.py
+++ b/solution.py
@@ -434,7 +434,7 @@
 
 TOK_CUTS = {"A": (0, 3456), "B": (3456, WIDE), "B1": (3456, 5376), "B2": (5376, WIDE), "F": (0, WIDE)}
 LAT_CUTS = {"A": (0, 1024), "B": (1024, LATW), "B1": (1024, 1664), "B2": (1664, LATW), "F": (0, LATW)}
-MIX_CUTS = {"A": (0, 96), "B": (96, 224), "B1": (96, 160), "B2": (160, 224), "F": (0, 224)}
+MIX_CUTS = {"A": (0, 112), "B": (112, 224), "B1": (112, 176), "B2": (176, 224), "F": (0, 224)}
 
 
 def relay_kernel(

time: 125 us -> 126 us (level)
  no operation moved by 1% of the time
where the time goes in v6:
time: 126 us
  Pallas kernels  125 us (99%)
  local copies, waits for them, and re-layouts  1.67 us (1%)
    pallas_call x1, Pallas kernels, per_device(): pl.pallas_call(functools.partial(relay_kernel, sections), name='relay', o...  125 us

profile of v6, /device:TPU:1, one launch (start us, length us, event | category | flops | bytes accessed | tf_op | source)
XLA Modules:
  0.0 126.2 jit_solution(2737459706365839772)
XLA Ops:
  0.0 124.6 %relay.1 = bf16[512,256]{1,0:T(8,128)(2,1)} custom-call(bf16[16,7168]{1,0:T(8,128)(2,1)} %bitcast.26, s32[2,16]{1,0:T(2,128)} %bitcast.28, f32[2,16]{1,0:T(2,128)} %bitcast.29, bf16[7168,128]{1,0:T(8,128)(2,1)} %bitcast.18, bf16[7168,128]{1,0:T(8,128)(2,1)} %bitcast.19, bf16[128,7168]{1,0:T(8,128)(2,1)} %bitcast.20, f32[1,7168]{1,0:T(1,128)} %gain_ref.1, ...), custom_call_target="tpu_custom_call" | custom-call | flops 12000000000 | bytes 12000000 | tf_op jit(solution)/shard_map/relay/pallas_call | solution.py:809
  124.6 1.7 %copy.18 = bf16[1,512,256]{2,1,0:T(8,128)(2,1)} copy(bf16[1,512,256]{2,1,0:T(8,128)(2,1)} %bitcast.17) | data formatting | bytes 524288
